TPU v7x, 32 devices: a whole 2x2x4 slice. The times are simulated.
32 devices in a mesh: dp: 16 (over z, x, core), mp: 2 (over y).
Axes of the slice: x: 2, y: 2, z: 4, core: 2. Of those that a mesh axis runs over, the one named last changes fastest.
Arguments:
- tokens: bfloat16 [8192, 768], P('dp'), may hold values from -6 to 6
- segment_ids: int32 [16, 512], P('dp'), may hold values from 0 to 5, never falling along the last dimension, each value on 1 to 256 neighbouring positions
- pad_flags: int32 [16, 512], P('dp'), may hold values 0 or 1
- query_weight: bfloat16 [768, 768], P(None, 'mp'), may hold values from -0.21875 to 0.21875
- query_bias: bfloat16 [768], P('mp'), may hold values from -1.5 to 1.5
- key_weight: bfloat16 [768, 768], P(None, 'mp'), may hold values from -0.21875 to 0.21875
- value_weight: bfloat16 [768, 768], P(None, 'mp'), may hold values from -0.21875 to 0.21875
- value_bias: bfloat16 [768], P('mp'), may hold values from -1.5 to 1.5
- output_weight: bfloat16 [768, 768], P('mp'), may hold values from -0.625 to 0.625
- output_bias: bfloat16 [768], replicated, may hold values from -1.5 to 1.5
- first_gain: bfloat16 [768], replicated, may hold values from 0.5 to 1.5
- first_shift: bfloat16 [768], replicated, may hold values from -1.5 to 1.5
- up_weight: bfloat16 [768, 3072], P(None, 'mp'), may hold values from -0.21875 to 0.21875
- up_bias: bfloat16 [3072], P('mp'), may hold values from -1.5 to 1.5
- down_weight: bfloat16 [3072, 768], P('mp'), may hold values from -0.21875 to 0.21875
- down_bias: bfloat16 [768], replicated, may hold values from -1.5 to 1.5
- second_gain: bfloat16 [768], replicated, may hold values from 0.5 to 1.5
- second_shift: bfloat16 [768], replicated, may hold values from -1.5 to 1.5
- term_weight: bfloat16 [768], replicated, may hold values from -0.21875 to 0.21875
- term_bias: bfloat16 [1], replicated, may hold values from -2.5 to 2.5
- hidden_cot: float32 [8192, 768], P('dp'), may hold values from -18 to 18
- term_cot: float32 [8192], P('dp'), may hold values from -6 to 6
Outputs:
- hidden: bfloat16 [8192, 768], P('dp')
- term_weights: float32 [8192], P('dp')
- tokens_grad: float32 [8192, 768], P('dp')
- queryweight_grad: float32 [768, 768], P(None, 'mp')
- querybias_grad: float32 [768], P('mp')
- keyweight_grad: float32 [768, 768], P(None, 'mp')
- valueweight_grad: float32 [768, 768], P(None, 'mp')
- valuebias_grad: float32 [768], P('mp')
- outputweight_grad: float32 [768, 768], P('mp')
- outputbias_grad: float32 [768], replicated
- firstgain_grad: float32 [768], replicated
- firstshift_grad: float32 [768], replicated
- upweight_grad: float32 [768, 3072], P(None, 'mp')
- upbias_grad: float32 [3072], P('mp')
- downweight_grad: float32 [3072, 768], P('mp')
- downbias_grad: float32 [768], replicated
- secondgain_grad: float32 [768], replicated
- secondshift_grad: float32 [768], replicated
- termweight_grad: float32 [768], replicated
- termbias_grad: float32 [1], replicated
All inputs are finite; a program needn't handle non-finite values. No bound on the sum of `pad_flags` on one device may be relied on, other than what follows from the above.
Results may differ from a plain program's by a relative error of at most 0.015.
Values sent between devices are 32-bit elements; how exact they have to be, the bound alone decides.
A program may use at most 128 MiB of HBM per device.

v0:
```python
from functools import partial

import jax
import jax.numpy as jnp
from jax import lax
from jax.sharding import PartitionSpec as P

HEAD_DIM = 64


EPS = 1e-06
ROWS_DIMS = (((0,), (0,)), ((), ()))
COLS_DIMS = (((1,), (1,)), ((), ()))


def layer_norm(resid, gain, shift):
    center = resid - jnp.mean(resid, axis=-1, keepdims=True)
    spread = jnp.mean(center * center, axis=-1, keepdims=True)
    return center * lax.rsqrt(spread + EPS) * gain + shift


def exact_gelu(upper):
    return jax.nn.gelu(upper, approximate=False)


def tail_piece(resid, gain, shift, weight, offset, keep):
    second = layer_norm(resid, gain, shift)
    term = jax.nn.softplus(jnp.sum(second * weight, axis=-1) + offset[0]) * keep
    return (second, term)


def row_mask(segment, padding):
    length = segment.shape[0]
    same = segment[:, None] == segment[None, :]
    diagonal = lax.broadcasted_iota(jnp.int32, (length, length), 0) == lax.broadcasted_iota(
        jnp.int32, (length, length), 1
    )
    return same & ((padding[None, :] == 0) | diagonal)


def row_scores(queries, key_rows, allowed):
    scale = queries.shape[-1] ** (-0.5)
    scores = (
        jnp.einsum("qhd,khd->hqk", queries, key_rows, preferred_element_type=jnp.float32) * scale
    )
    return jnp.where(allowed[None], scores, -1000000000.0)


def attend_forward(items):
    queries, key_rows, values, segment, padding = items
    scores = row_scores(queries, key_rows, row_mask(segment, padding))
    maxima = jnp.max(scores, axis=-1, keepdims=True)
    expo = jnp.exp(scores - maxima)
    totals = jnp.sum(expo, axis=-1, keepdims=True)
    probs = expo / totals
    context = jnp.einsum(
        "hqk,khd->qhd", probs.astype(jnp.bfloat16), values, preferred_element_type=jnp.float32
    )
    return (context.astype(jnp.bfloat16), maxima + jnp.log(totals))


def attend_backward(items):
    queries, key_rows, values, segment, padding, logsum, dcontext = items
    scale = queries.shape[-1] ** (-0.5)
    scores = row_scores(queries, key_rows, row_mask(segment, padding))
    probs = jnp.exp(scores - logsum)
    dvalues = jnp.einsum(
        "hqk,qhd->khd", probs.astype(jnp.bfloat16), dcontext, preferred_element_type=jnp.float32
    )
    dprobs = jnp.einsum("qhd,khd->hqk", dcontext, values, preferred_element_type=jnp.float32)
    inner = jnp.sum(dprobs * probs, axis=-1, keepdims=True)
    dscores = (probs * (dprobs - inner)).astype(jnp.bfloat16)
    dqueries = (
        jnp.einsum("hqk,khd->qhd", dscores, key_rows, preferred_element_type=jnp.float32) * scale
    )
    dkeys = jnp.einsum("hqk,qhd->khd", dscores, queries, preferred_element_type=jnp.float32) * scale
    return (dqueries.astype(jnp.bfloat16), dkeys.astype(jnp.bfloat16), dvalues.astype(jnp.bfloat16))


def per_device(
    tokens,
    segment_ids,
    pad_flags,
    query_weight,
    query_bias,
    key_weight,
    value_weight,
    value_bias,
    output_weight,
    output_bias,
    first_gain,
    first_shift,
    up_weight,
    up_bias,
    down_weight,
    down_bias,
    second_gain,
    second_shift,
    term_weight,
    term_bias,
    hidden_cot,
    term_cot,
):
    rows, length = segment_ids.shape
    count = rows * length
    local = query_weight.shape[1]
    heads = local // HEAD_DIM

    def split_heads(block):
        return block.reshape(rows, length, heads, HEAD_DIM)

    queries = (
        jnp.dot(tokens, query_weight, preferred_element_type=jnp.float32)
        + query_bias.astype(jnp.float32)
    ).astype(jnp.bfloat16)
    key_rows = jnp.dot(tokens, key_weight, preferred_element_type=jnp.float32).astype(jnp.bfloat16)
    values = (
        jnp.dot(tokens, value_weight, preferred_element_type=jnp.float32)
        + value_bias.astype(jnp.float32)
    ).astype(jnp.bfloat16)
    context, logsum = lax.map(
        attend_forward,
        (split_heads(queries), split_heads(key_rows), split_heads(values), segment_ids, pad_flags),
    )
    context = context.reshape(count, local)
    attn_total = lax.psum(jnp.dot(context, output_weight, preferred_element_type=jnp.float32), "mp")
    resid_one = tokens.astype(jnp.float32) + attn_total + output_bias.astype(jnp.float32)
    first, first_back = jax.vjp(
        layer_norm, resid_one, first_gain.astype(jnp.float32), first_shift.astype(jnp.float32)
    )
    first_low = first.astype(jnp.bfloat16)
    upper = jnp.dot(first_low, up_weight, preferred_element_type=jnp.float32) + up_bias.astype(
        jnp.float32
    )
    active, gelu_back = jax.vjp(exact_gelu, upper)
    active_low = active.astype(jnp.bfloat16)
    branch_total = lax.psum(
        jnp.dot(active_low, down_weight, preferred_element_type=jnp.float32), "mp"
    )
    resid_two = first + branch_total + down_bias.astype(jnp.float32)
    keep_flag = 1.0 - pad_flags.reshape(count).astype(jnp.float32)
    (second, term_weights), tail_back = jax.vjp(
        partial(tail_piece, keep=keep_flag),
        resid_two,
        second_gain.astype(jnp.float32),
        second_shift.astype(jnp.float32),
        term_weight.astype(jnp.float32),
        term_bias.astype(jnp.float32),
    )
    dresid_two, secondgain_grad, secondshift_grad, termweight_grad, termbias_grad = tail_back(
        (hidden_cot, term_cot)
    )
    dbranch = dresid_two.astype(jnp.bfloat16)
    downbias_grad = jnp.sum(dbranch.astype(jnp.float32), axis=0)
    downweight_grad = lax.dot_general(
        active_low, dbranch, ROWS_DIMS, preferred_element_type=jnp.float32
    )
    dactive = lax.dot_general(dbranch, down_weight, COLS_DIMS, preferred_element_type=jnp.float32)
    (dupper,) = gelu_back(dactive)
    dupper_low = dupper.astype(jnp.bfloat16)
    upbias_grad = jnp.sum(dupper_low.astype(jnp.float32), axis=0)
    upweight_grad = lax.dot_general(
        first_low, dupper_low, ROWS_DIMS, preferred_element_type=jnp.float32
    )
    first_part = lax.dot_general(
        dupper_low, up_weight, COLS_DIMS, preferred_element_type=jnp.float32
    )
    dfirst = dresid_two + lax.psum(first_part, "mp")
    dresid_one, firstgain_grad, firstshift_grad = first_back(dfirst)
    dattn = dresid_one.astype(jnp.bfloat16)
    outputbias_grad = jnp.sum(dattn.astype(jnp.float32), axis=0)
    outputweight_grad = lax.dot_general(
        context, dattn, ROWS_DIMS, preferred_element_type=jnp.float32
    )
    dcontext = lax.dot_general(
        dattn, output_weight, COLS_DIMS, preferred_element_type=jnp.float32
    ).astype(jnp.bfloat16)
    dqueries, dkeys, dvalues = lax.map(
        attend_backward,
        (
            split_heads(queries),
            split_heads(key_rows),
            split_heads(values),
            segment_ids,
            pad_flags,
            logsum,
            split_heads(dcontext),
        ),
    )
    dqueries = dqueries.reshape(count, local)
    dkeys = dkeys.reshape(count, local)
    dvalues = dvalues.reshape(count, local)
    queryweight_grad = lax.dot_general(
        tokens, dqueries, ROWS_DIMS, preferred_element_type=jnp.float32
    )
    keyweight_grad = lax.dot_general(tokens, dkeys, ROWS_DIMS, preferred_element_type=jnp.float32)
    valueweight_grad = lax.dot_general(
        tokens, dvalues, ROWS_DIMS, preferred_element_type=jnp.float32
    )
    querybias_grad = jnp.sum(dqueries.astype(jnp.float32), axis=0)
    valuebias_grad = jnp.sum(dvalues.astype(jnp.float32), axis=0)
    token_part = lax.dot_general(
        dqueries, query_weight, COLS_DIMS, preferred_element_type=jnp.float32
    )
    token_part = token_part + lax.dot_general(
        dkeys, key_weight, COLS_DIMS, preferred_element_type=jnp.float32
    )
    token_part = token_part + lax.dot_general(
        dvalues, value_weight, COLS_DIMS, preferred_element_type=jnp.float32
    )
    tokens_grad = dresid_one + lax.psum(token_part, "mp")
    (
        queryweight_grad,
        querybias_grad,
        keyweight_grad,
        valueweight_grad,
        valuebias_grad,
        outputweight_grad,
        outputbias_grad,
        firstgain_grad,
        firstshift_grad,
        upweight_grad,
        upbias_grad,
        downweight_grad,
        downbias_grad,
        secondgain_grad,
        secondshift_grad,
        termweight_grad,
        termbias_grad,
    ) = lax.psum(
        (
            queryweight_grad,
            querybias_grad,
            keyweight_grad,
            valueweight_grad,
            valuebias_grad,
            outputweight_grad,
            outputbias_grad,
            firstgain_grad,
            firstshift_grad,
            upweight_grad,
            upbias_grad,
            downweight_grad,
            downbias_grad,
            secondgain_grad,
            secondshift_grad,
            termweight_grad,
            termbias_grad,
        ),
        "dp",
    )
    return (
        second.astype(jnp.bfloat16),
        term_weights,
        tokens_grad,
        queryweight_grad,
        querybias_grad,
        keyweight_grad,
        valueweight_grad,
        valuebias_grad,
        outputweight_grad,
        outputbias_grad,
        firstgain_grad,
        firstshift_grad,
        upweight_grad,
        upbias_grad,
        downweight_grad,
        downbias_grad,
        secondgain_grad,
        secondshift_grad,
        termweight_grad,
        termbias_grad,
    )


def solution(mesh):
    return jax.shard_map(
        per_device,
        mesh=mesh,
        in_specs=(
            P("dp", None),
            P("dp", None),
            P("dp", None),
            P(None, "mp"),
            P("mp"),
            P(None, "mp"),
            P(None, "mp"),
            P("mp"),
            P("mp", None),
            P(),
            P(),
            P(),
            P(None, "mp"),
            P("mp"),
            P("mp", None),
            P(),
            P(),
            P(),
            P(),
            P(),
            P("dp", None),
            P("dp"),
        ),
        out_specs=(
            P("dp", None),
            P("dp"),
            P("dp", None),
            P(None, "mp"),
            P("mp"),
            P(None, "mp"),
            P(None, "mp"),
            P("mp"),
            P("mp", None),
            P(),
            P(),
            P(),
            P(None, "mp"),
            P("mp"),
            P("mp", None),
            P(),
            P(),
            P(),
            P(),
            P(),
        ),
        check_vma=False,
    )
```

profile of v0, /device:TPU:0, one launch (start us, length us, event | category | flops | bytes accessed | tf_op | source)
XLA Modules:
  0.0 569.0 jit_solution(4457916215120252992)
XLA Ops:
  9.6 1.8 convolution_convert_fusion.1
  15.6 1.7 copy-done.2
  19.4 1.7 fusion.42
  22.4 53.1 %all-reduce.8.cloned.1.call-done = f32[512,768]{1,0:T(8,128)} async-done(((f32[512,768]{1,0:T(8,128)}), f32[512,768]{1,0:T(8,128)}) %all-reduce.8.cloned.1.call-update) | async-done | bytes 1572880 | tf_op jit(solution)/shard_map/psum | solution.py:126
  78.0 9.3 %multiply_convert_fusion.1 = (bf16[512,1536]{1,0:T(8,128)(2,1)S(1)}, f32[512,1536]{1,0:T(8,128)}, f32[512,1536]{1,0:T(8,128)}) fusion(f32[1536]{0:T(1024)S(1)} %copy-done.62, bf16[768,1536]{1,0:T(8,128)(2,1)S(1)} %copy-done, f32[512,768]{1,0:T(8,128)S(1)} %get-tuple-element.139, f32[768]{0:T(1024)S(1)} %copy-done.54, f32[768]{0:T(1024)S(1)} %convert_element_type.135, ...), kind=kOutput, calls=%fused_computation.15 | convolution fusion | flops 1261830144 | bytes 11812864 | tf_op jit(solution)/shard_map/dot_general | solution.py:132
  88.5 2.5 fusion.43
  96.2 46.5 %all-reduce.10.cloned.1.call-done = f32[512,768]{1,0:T(8,128)} async-done(((f32[512,768]{1,0:T(8,128)}), f32[512,768]{1,0:T(8,128)}) %all-reduce.10.cloned.1.call-update) | async-done | bytes 1572880 | tf_op jit(solution)/shard_map/psum | solution.py:137
  142.7 2.5 fusion.38
  147.6 2.5 multiply_reduce_fusion.2
  153.4 2.9 convert_reduce_fusion
  157.4 2.6 fusion.44
  161.2 50.4 %all-reduce.12.cloned.1.call-done = f32[512,768]{1,0:T(8,128)} async-done(((f32[512,768]{1,0:T(8,128)}), f32[512,768]{1,0:T(8,128)}) %all-reduce.12.cloned.1.call-update) | async-done | bytes 1572880 | tf_op jit(solution)/shard_map/psum | solution.py:168
  211.7 3.4 multiply_reduce_fusion.3
  219.2 1.9 multiply_convert_fusion
  223.5 1.8 convert_reduce_fusion.3
  227.0 1.8 add_add_fusion.2
  229.2 5.3 fusion.48
  234.5 3.8 fusion.31
  245.2 62.5 %all-reduce = (f32[384]{0:T(512)}, f32[384]{0:T(512)}, f32[768]{0:T(1024)}, f32[768]{0:T(1024)}, f32[768]{0:T(1024)}, /*index=5*/f32[1536]{0:T(1024)}, f32[768]{...) all-reduce(f32[384]{0:T(512)S(1)} %reduce_sum.252, ...), channel_id=1, replica_groups=mesh['dp'=16,'mp'=2] {'dp'}, use_global_device_ids=true, to_apply=%region_18.19 | all-reduce | flops 7681 | bytes 61448 | tf_op jit(solution)/shard_map/psum | solution.py:230
  307.7 2.8 add_add_fusion.5
  310.6 236.4 %all-reduce.16.cloned.1.call-done = (f32[768,384]{0,1:T(8,128)}, f32[768,384]{0,1:T(8,128)}, f32[768,384]{0,1:T(8,128)}, f32[384,768]{1,0:T(8,128)}, f32[768,1536]{1,0:T(8,128)}, /*index=5*/f32[1536,768]{1,0:T(8,128)}) async-done(((f32[768,384]{0,1:T(8,128)}, f32[768,384]{0,1:T(8,128)}, f32[768,384]{0,1:T(8,128)}, f32[384,768]{1,0:T(8,128)}, f32[768,1536]{1,0:T(8,128)}, /*index=5*/f32[1536,768]{1,0:T(8,128)}), ...) | async-done | bytes 14155792 | tf_op jit(solution)/shard_map/psum | solution.py:230
  547.0 2.7 copy.46
  553.5 5.5 copy.65
  559.1 2.4 copy.66
  (227 shorter events, 45.7 us)
Async XLA Ops:
  7.2 70.4 %copy-start = (bf16[768,1536]{1,0:T(8,128)(2,1)S(1)}, bf16[768,1536]{1,0:T(8,128)(2,1)}, u32[]{:S(2)}) copy-start(bf16[768,1536]{1,0:T(8,128)(2,1)} %param.34) | copy-start | bytes 7077892
  7.2 68.3 %all-reduce.8.cloned.1.call-start = ((), (), s32[]{:S(2)}) async-start(), calls=%async_computation | async-start | bytes 3145728 | tf_op jit(solution)/shard_map/psum | solution.py:126
  21.1 121.5 %all-reduce.10.cloned.1.call-start = ((), (), s32[]{:S(2)}) async-start(), calls=%async_computation.1 | async-start | bytes 3145728 | tf_op jit(solution)/shard_map/psum | solution.py:137
  22.4 120.3 %copy-start.34 = (f32[768]{0:T(1024)}, f32[768]{0:T(1024)S(1)}, u32[]{:S(2)}) copy-start(f32[768]{0:T(1024)S(1)} %convert_element_type.135) | copy-start | bytes 9220
  77.2 10.1 %copy-start.3 = (f32[512,768]{1,0:T(8,128)}, f32[512,768]{1,0:T(8,128)S(1)}, u32[]{:S(2)}) copy-start(f32[512,768]{1,0:T(8,128)S(1)} %get-tuple-element.139) | copy-start | bytes 4718596
  77.2 65.5 %copy-start.37 = (f32[512]{0:T(512)}, f32[512]{0:T(512)S(1)}, u32[]{:S(2)}) copy-start(f32[512]{0:T(512)S(1)} %broadcast_multiply_fusion.1) | copy-start | bytes 6148
  77.5 9.8 %copy-start.44 = (f32[512]{0:T(512)}, f32[512]{0:T(512)S(1)}, u32[]{:S(2)}) copy-start(f32[512]{0:T(512)S(1)} %multiply_reduce_fusion.8) | copy-start | bytes 6148
  78.0 9.4 %copy-start.41 = (f32[512]{0:T(512)}, f32[512]{0:T(512)S(1)}, u32[]{:S(2)}) copy-start(f32[512]{0:T(512)S(1)} %fusion.28) | copy-start | bytes 6148
  78.0 10.5 %copy-start.72 = (bf16[1536,768]{1,0:T(8,128)(2,1)S(1)}, bf16[1536,768]{1,0:T(8,128)(2,1)}, u32[]{:S(2)}) copy-start(bf16[1536,768]{1,0:T(8,128)(2,1)} %param.36) | copy-start | bytes 7077892
  91.0 120.6 %all-reduce.12.cloned.1.call-start = ((), (), s32[]{:S(2)}) async-start(), calls=%async_computation.2 | async-start | bytes 3145728 | tf_op jit(solution)/shard_map/psum | solution.py:168
  160.0 51.7 %copy-start.4 = (f32[512,768]{1,0:T(8,128)S(1)}, f32[512,768]{1,0:T(8,128)}, u32[]{:S(2)}) copy-start(f32[512,768]{1,0:T(8,128)} %copy-done.3) | copy-start | bytes 4718596
  160.0 51.7 %copy-start.35 = (f32[768]{0:T(1024)S(1)}, f32[768]{0:T(1024)}, u32[]{:S(2)}) copy-start(f32[768]{0:T(1024)} %copy-done.34) | copy-start | bytes 9220
  160.0 51.7 %copy-start.38 = (f32[512]{0:T(512)S(1)}, f32[512]{0:T(512)}, u32[]{:S(2)}) copy-start(f32[512]{0:T(512)} %copy-done.37) | copy-start | bytes 6148
  160.0 51.7 %copy-start.42 = (f32[512]{0:T(512)S(1)}, f32[512]{0:T(512)}, u32[]{:S(2)}) copy-start(f32[512]{0:T(512)} %copy-done.41) | copy-start | bytes 6148
  160.0 51.7 %copy-start.49 = (f32[512]{0:T(512)S(1)}, f32[512]{0:T(512)}, u32[]{:S(2)}) copy-start(f32[512]{0:T(512)} %copy-done.48) | copy-start | bytes 6148
  160.0 147.7 %all-reduce.14.cloned.1.call-start = ((), (), s32[]{:S(2)}) async-start(), calls=%async_computation.3 | async-start | bytes 3145728 | tf_op jit(solution)/shard_map/psum | solution.py:211
  161.2 53.9 %copy-start.45 = (f32[512]{0:T(512)S(1)}, f32[512]{0:T(512)}, u32[]{:S(2)}) copy-start(f32[512]{0:T(512)} %copy-done.44) | copy-start | bytes 6148
  211.7 6.2 %slice-start = ((s8[6291456]{0:T(1024)(128)(4,1)}), s8[4194304]{0:T(1024)(128)(4,1)S(1)}, s32[]{:S(2)}) async-start(s8[6291456]{0:T(1024)(128)(4,1)} %bitcast.74), calls=%async_computation.5 | async-start | bytes 8388608
  228.8 5.7 %copy-start.36 = (f32[768]{0:T(1024)S(1)}, f32[768]{0:T(1024)}, u32[]{:S(2)}) copy-start(f32[768]{0:T(1024)} %copy-done.34) | copy-start | bytes 9220
  228.8 5.7 %copy-start.39 = (f32[512]{0:T(512)S(1)}, f32[512]{0:T(512)}, u32[]{:S(2)}) copy-start(f32[512]{0:T(512)} %copy-done.37) | copy-start | bytes 6148
  228.8 318.1 %all-reduce.16.cloned.1.call-start = ((), (), s32[]{:S(2)}) async-start(), calls=%async_computation.4 | async-start | bytes 28311552 | tf_op jit(solution)/shard_map/psum | solution.py:230
  244.4 63.4 %copy-start.6 = (f32[512,768]{1,0:T(8,128)S(1)}, f32[512,768]{1,0:T(8,128)}, u32[]{:S(2)}) copy-start(f32[512,768]{1,0:T(8,128)} %copy-done.5) | copy-start | bytes 4718596
  244.4 63.3 %copy-start.47 = (f32[512]{0:T(512)S(1)}, f32[512]{0:T(512)}, u32[]{:S(2)}) copy-start(f32[512]{0:T(512)} %copy-done.46) | copy-start | bytes 6148
  552.5 6.5 %slice-start.2 = ((s8[4718592]{0:T(1024)(128)(4,1)}), s8[4194304]{0:T(1024)(128)(4,1)S(1)}, s32[]{:S(2)}) async-start(s8[4718592]{0:T(1024)(128)(4,1)} %bitcast.76), calls=%async_computation.7 | async-start | bytes 8388608
  (63 other events, 126.7 us)
Sparse Core Ops, SparseCore 0:
  21.3 54.1 all-reduce.7
  91.1 51.4 all-reduce.9
  160.1 51.4 all-reduce.11
  228.9 51.4 all-reduce.13
  286.6 260.3 all-reduce.15
where the time goes:
time: 570 us; the launch traced here: 569 us
  waiting for transfers between devices  386 us (68%)
  blocking collectives  62.5 us (11%)
  matrix products  48.4 us (8%)
  other arithmetic  29.5 us (5%)
  local copies, waits for them, and re-layouts  25.9 us (5%)
  between operations  15.2 us (3%)
    psum x1, waiting for transfers between devices, per_device(): lax.psum((queryweight_grad, querybias_grad, keyweight_grad, valueweight_g...  236 us
    psum x1, blocking collectives, per_device(): lax.psum((queryweight_grad, querybias_grad, keyweight_grad, valueweight_g...  62.5 us
    psum x1, waiting for transfers between devices, per_device(): lax.psum(jnp.dot(context, output_weight, preferred_element_type=jnp.float...  53.1 us
    psum x1, waiting for transfers between devices, per_device(): dfirst = dresid_two + lax.psum(first_part, 'mp')  50.4 us
    psum x1, waiting for transfers between devices, per_device(): lax.psum(jnp.dot(active_low, down_weight, preferred_element_type=jnp.floa...  46.5 us
    unnamed x170, local copies, waits for them, and re-layouts  25.8 us
  transfers between devices with their start and end apart: 5, of which 4 were waited for; matrix products, arithmetic and copies ran while one was open for 4% of the time, Pallas kernels for 0%

commit v1 on v0

v1 whole, which is shorter than its diff:
```python
from functools import partial

import jax
import jax.numpy as jnp
from jax import lax
from jax.experimental import pallas as pl
from jax.experimental.pallas import tpu as pltpu
from jax.sharding import PartitionSpec as P

HEAD_DIM = 64
EPS = 1e-06
GROUP = 16
RING = 8
BATCHES = 6
MESH = pl.DeviceIdType.MESH
bf16, f32 = jnp.bfloat16, jnp.float32

V_QV, V_OB, V_G1, V_S1, V_DB, V_G2, V_S2, V_TW, V_TB = range(9)
G_QV, G_OB, G_G1, G_S1, G_UB0, G_UB1, G_DB, G_G2, G_S2, G_TW, G_TB = range(11)


def nn(a, b):
    return jnp.dot(a, b, preferred_element_type=f32)


def nt(a, b):
    return lax.dot_general(a, b, (((1,), (1,)), ((), ())), preferred_element_type=f32)


def tn(a, b):
    return lax.dot_general(a, b, (((0,), (0,)), ((), ())), preferred_element_type=f32)


def colsum(v):
    return jnp.sum(v, axis=0, keepdims=True)


def rowmean(v):
    return jnp.mean(v, axis=-1, keepdims=True)


def kernel(
    tokens, seg, pad, tcot, vec, ubv, wq, wk, wv, wo, wu, wd, hcot,
    o_hid, o_term, o_tok, o_wq, o_wk, o_wv, o_wo, o_wu, o_wd, o_sm,
    tok_v, wq_v, wk_v, wv_v, wo_v, woo_v, wu_v, wd_v, hc,
    kn, vn, kT, vT, qz, qTz, pm, ctxT, xh, rs, fl, gp, act, bs, br, fr, db, du,
    dcz, dcTz, dsb, dqT, dq, dk, dv, hid, col, trm, sm, smr, G, S, R,
    ld_sem, out_sem, y_s, y_r, wx_s, wx_r, ws_s, ws_r, sm_s, sm_r,
    sib_s, sib_r, rs_s, rs_r, ag_s, ag_r, fw_s, fw_r, free_sib, free_ring,
):
    T, D = tokens.shape
    L, F = wq.shape[1], wu.shape[1]
    NP = L // 128
    CH, PC, FB = T // 2, T // 4, 512
    NPC = T // PC
    SUB = G.shape[0] // BATCHES
    HALF, CK = SUB // 2, SUB // 2 // RING

    me, mp = lax.axis_index("dp"), lax.axis_index("mp")
    base, rank = me // GROUP * GROUP, me % GROUP
    core, chip = rank % 2, rank // 2
    x, z = chip % 2, chip // 2
    pos = jnp.where(x == 0, z, RING - 1 - z)
    vp = jnp.where(core == 0, pos, (RING - pos) % RING)
    vps = (RING - vp) % RING

    def at_vp(v):
        p = jnp.where(core == 0, v, (RING - v) % RING)
        c = jnp.where(p < RING // 2, 2 * p, 2 * (RING - 1 - p) + 1)
        return (base + 2 * c + core, mp)

    def at_xz(ax, az):
        return (base + 2 * (2 * az + ax) + core, mp)

    YN = (me, 1 - mp)
    SIB = (base + 2 * chip + 1 - core, mp)
    NXT, PRV = at_vp((vp + 1) % RING), at_vp((vp + RING - 1) % RING)
    XN = at_xz(1 - x, z)
    Z1 = at_xz(x, z // 2 * 2 + 1 - z % 2)
    Z2 = at_xz(x, (z + 2) % 4)

    def rc(src, dst, ss, rr, dev):
        return pltpu.make_async_remote_copy(
            src_ref=src, dst_ref=dst, send_sem=ss, recv_sem=rr, device_id=dev, device_id_type=MESH
        )

    pairs = [
        (tokens, tok_v), (wq, wq_v), (wk, wk_v), (wv, wv_v), (wo, wo_v), (wu, wu_v), (wd, wd_v), (hcot, hc),
    ]
    loads = [pltpu.make_async_copy(a, b, ld_sem.at[i]) for i, (a, b) in enumerate(pairs)]
    for c in loads:
        c.start()
    L_TOK, L_WQ, L_WK, L_WV, L_WO, L_WU, L_WD, L_HC = loads

    peers = (YN, SIB, NXT, PRV, XN, Z1, Z2)
    bar = pltpu.get_barrier_semaphore()
    for d in peers:
        pl.semaphore_signal(bar, inc=1, device_id=d, device_id_type=MESH)
    pl.semaphore_wait(bar, len(peers))

    r_first = 1 * F
    r_wor = r_first + T
    r_wos = r_wor + L
    r_bias = 2 * F
    r_cs = r_bias + T
    r_cr = r_cs + L
    SH = L // 4

    L_WO.wait()
    share = pl.multiple_of((2 * x + core) * SH, SH)
    share_x = pl.multiple_of((2 * (1 - x) + core) * SH, SH)
    share_s = pl.multiple_of((2 * x + 1 - core) * SH, SH)
    share_sx = pl.multiple_of((2 * (1 - x) + 1 - core) * SH, SH)
    G[r_wos : r_wos + SH, :] = wo_v[pl.ds(share, SH), :].astype(f32)

    def wor(s):
        return G.at[pl.ds(pl.multiple_of(r_wor + s, 32), SH)]

    wo_y = rc(G.at[pl.ds(r_wos, SH)], wor(share), y_s.at[0], y_r.at[0], YN)
    wo_y.start()
    wo_x = rc(wor(share), wor(share), wx_s.at[0], wx_r.at[0], XN)
    wo_x_in = rc(wor(share_x), wor(share_x), wx_s.at[0], wx_r.at[0], XN)
    wo_f = [
        rc(wor(share), wor(share), ws_s.at[0], ws_r.at[0], SIB),
        rc(wor(share_x), wor(share_x), ws_s.at[1], ws_r.at[1], SIB),
    ]
    wo_f_in = [
        rc(wor(share_s), wor(share_s), ws_s.at[0], ws_r.at[0], SIB),
        rc(wor(share_sx), wor(share_sx), ws_s.at[1], ws_r.at[1], SIB),
    ]

    L_TOK.wait()
    L_WQ.wait()
    lane = lax.broadcasted_iota(jnp.int32, (T, L), 1)
    odd = (lane // HEAD_DIM) % 2
    qv = (nn(tok_v[...], wq_v[...]) + vec[V_QV : V_QV + 1, 0:L]).astype(bf16).astype(f32) * (HEAD_DIM**-0.5)
    for par in range(2):
        one = jnp.where(odd == par, qv, 0.0).astype(bf16)
        qz[par * T : (par + 1) * T, :] = one
        qTz[par * L : (par + 1) * L, :] = one.T
    L_WK.wait()
    kv = nn(tok_v[...], wk_v[...]).astype(bf16)
    kn[...] = kv
    kT[...] = kv.T
    L_WV.wait()
    vv = (nn(tok_v[...], wv_v[...]) + vec[V_QV : V_QV + 1, L : 2 * L]).astype(bf16)
    vn[...] = vv
    vT[...] = vv.T

    segf, padf = seg[...].astype(f32), pad[...].astype(f32)
    rows8 = jnp.concatenate([segf, padf, tcot[...], jnp.zeros((5, T), f32)], axis=0)
    col[...] = rows8.T
    for qc in range(2):
        ki = lax.broadcasted_iota(jnp.int32, (T, CH), 0)
        qi = lax.broadcasted_iota(jnp.int32, (T, CH), 1) + qc * CH
        same = col[:, 0:1] == segf[:, qc * CH : (qc + 1) * CH]
        allowed = same & ((col[:, 1:2] == 0.0) | (ki == qi))
        G[r_bias : r_bias + T, qc * CH : (qc + 1) * CH] = jnp.where(allowed, 0.0, -1e9)

    def ctx_copy(qc):
        cols = pl.ds(qc * CH, CH)
        return rc(
            G.at[pl.ds(r_cs, L), cols], G.at[pl.ds(r_cr, L), cols], y_s.at[1 + qc], y_r.at[1 + qc], YN
        )

    def attend(qc):
        cols = pl.ds(qc * CH, CH)

        def body(hp, _):
            blk = pl.ds(pl.multiple_of(hp * 128, 128), 128)
            for par in range(2):
                qrows = pl.ds(pl.multiple_of(par * L + hp * 128, 128), 128)
                head = pl.multiple_of(hp * 128 + par * HEAD_DIM, HEAD_DIM)
                s = nn(kn[:, blk], qTz[qrows, cols]) + G[r_bias : r_bias + T, cols]
                e = jnp.exp(s - jnp.max(s, axis=0, keepdims=True))
                p = (e * (1.0 / colsum(e))).astype(bf16)
                pm[hp, :, pl.ds(par * T + qc * CH, CH)] = p
                c = nn(vT[pl.ds(head, HEAD_DIM), :], p).astype(bf16)
                ctxT[pl.ds(head, HEAD_DIM), cols] = c
                G[pl.ds(pl.multiple_of(r_cs + head, HEAD_DIM), HEAD_DIM), cols] = c.astype(f32)
            return 0

        lax.fori_loop(0, NP, body, 0)

    attend(0)
    ctx_copy(0).start()
    wo_y.wait_recv()
    wo_x.start()
    wo_f[0].start()
    attend(1)
    ctx_copy(1).start()
    wo_x_in.wait_recv()
    wo_f[1].start()

    def attn_ln(qc):
        c0 = qc * CH
        cols = pl.ds(c0, CH)
        ctx_copy(qc).wait_recv()
        other = G[r_cr : r_cr + L, cols].astype(bf16)
        bs[c0 : c0 + CH, :] = tn(ctxT[:, cols], wo_v[...]) + tn(other, woo_v[...])

        def body(i, _):
            rows = pl.ds(pl.multiple_of(c0 + i * PC, PC), PC)
            res = tok_v[rows, :].astype(f32) + bs[rows, :] + vec[V_OB : V_OB + 1, :]
            cen = res - rowmean(res)
            rstd = lax.rsqrt(rowmean(cen * cen) + EPS)
            xv = cen * rstd
            xh[rows, :] = xv
            rs[rows, :] = jnp.broadcast_to(rstd, (PC, 128))
            first = xv * vec[V_G1 : V_G1 + 1, :] + vec[V_S1 : V_S1 + 1, :]
            G[pl.ds(pl.multiple_of(r_first + c0 + i * PC, PC), PC), :] = first
            fl[rows, :] = first.astype(bf16)
            return 0

        lax.fori_loop(0, CH // PC, body, 0)

    def ffn(qc):
        rows = pl.ds(qc * CH, CH)
        bs[rows, :] = jnp.zeros((CH, D), f32)

        def body(fb, _):
            cols = pl.ds(pl.multiple_of(fb * FB, FB), FB)
            u = nn(fl[rows, :], wu_v[:, cols]) + ubv[:, cols]
            ph = 0.5 + 0.5 * lax.erf(u * 0.7071067811865476)
            a = (u * ph).astype(bf16)
            act[rows, cols] = a
            gp[rows, cols] = (ph + u * (jnp.exp(-0.5 * u * u) * 0.3989422804014327)).astype(bf16)
            bs[rows, :] += nn(a, wd_v[cols, :])
            return 0

        lax.fori_loop(0, F // FB, body, 0)

    def piece(buf, i):
        return buf.at[pl.ds(pl.multiple_of(i * PC, PC), PC)]

    def y_piece(dst, first_sem, i):
        return rc(piece(bs, i), piece(dst, i), y_s.at[first_sem + i], y_r.at[first_sem + i], YN)

    Y_BR, Y_FP, Y_TP = 3, 3 + NPC, 3 + 2 * NPC

    for c in wo_f_in:
        c.wait_recv()
    woo_v[...] = G[r_wor : r_wor + L, :].astype(bf16)
    L_WU.wait()
    L_WD.wait()
    for qc in range(2):
        attn_ln(qc)
        ffn(qc)
        for i in range(2 * qc, 2 * qc + 2):
            y_piece(br, Y_BR, i).start()
    wo_y.wait_send()
    wo_x.wait_send()
    for c in wo_f:
        c.wait_send()
    for qc in range(2):
        ctx_copy(qc).wait_send()

    sm[0] = jnp.zeros((16, D), f32)
    L_HC.wait()

    def tail(i, _):
        rows = pl.ds(pl.multiple_of(i * PC, PC), PC)
        y_piece(br, Y_BR, i).wait_recv()
        first = G[pl.ds(pl.multiple_of(r_first + i * PC, PC), PC), :]
        res = first + (bs[rows, :] + br[rows, :]) + vec[V_DB : V_DB + 1, :]
        cen = res - rowmean(res)
        rstd = lax.rsqrt(rowmean(cen * cen) + EPS)
        xv = cen * rstd
        g2 = vec[V_G2 : V_G2 + 1, :]
        tw = vec[V_TW : V_TW + 1, :]
        second = xv * g2 + vec[V_S2 : V_S2 + 1, :]
        hid[rows, :] = second.astype(bf16)
        v = jnp.sum(second * tw, axis=-1, keepdims=True) + vec[V_TB : V_TB + 1, 0:1]
        keep = 1.0 - col[rows, 1:2]
        soft = jnp.maximum(v, 0.0) + jnp.log1p(jnp.exp(-jnp.abs(v)))
        trm[rows, :] = jnp.broadcast_to(soft * keep, (PC, 8))
        dterm = col[rows, 2:3] * keep * lax.logistic(v)
        dsec = hc[rows, :] + dterm * tw
        sm[0, G_G2 : G_G2 + 1, :] += colsum(dsec * xv)
        sm[0, G_S2 : G_S2 + 1, :] += colsum(dsec)
        sm[0, G_TW : G_TW + 1, :] += colsum(dterm * second)
        sm[0, G_TB : G_TB + 1, :] += jnp.broadcast_to(colsum(dterm), (1, D))
        dx = dsec * g2
        dr = rstd * (dx - rowmean(dx) - xv * rowmean(dx * xv))
        hc[rows, :] = dr
        low = dr.astype(bf16)
        db[rows, :] = low
        sm[0, G_DB : G_DB + 1, :] += colsum(low.astype(f32))
        return 0

    lax.fori_loop(0, NPC, tail, 0)

    def chunk(b, j):
        return pl.ds(pl.multiple_of(b * SUB + core * HALF + j * CK, 8), CK)

    def chunk_s(b, j):
        return pl.ds(pl.multiple_of(b * SUB + (1 - core) * HALF + j * CK, 8), CK)

    def mine(b, j):
        return G[chunk(b, j), :] + S[b, pl.ds(pl.multiple_of(j * CK, 8), CK), :]

    def sib_copy(b):
        src = G.at[pl.ds(pl.multiple_of(b * SUB + (1 - core) * HALF, 8), HALF)]
        return rc(src, S.at[b], sib_s.at[b], sib_r.at[b], SIB)

    def rs_copy(b, k):
        src = G.at[chunk(b, vp)] if k == 0 else R.at[b, k - 1]
        return rc(src, R.at[b, k], rs_s.at[b, k], rs_r.at[b, k], NXT)

    def ag_copy(b, k):
        rows = chunk(b, (vp + 1 - k + RING) % RING)
        return rc(G.at[rows], G.at[rows], ag_s.at[b, k], ag_r.at[b, k], NXT)

    def ag_in(b, k):
        rows = chunk(b, (vp - k + RING) % RING)
        return rc(G.at[rows], G.at[rows], ag_s.at[b, k], ag_r.at[b, k], NXT)

    def fw_copy(b, k):
        rows = chunk(b, (vp + 1 - k + RING) % RING)
        return rc(G.at[rows], G.at[rows], fw_s.at[b, k], fw_r.at[b, k], SIB)

    def fw_in(b, k):
        rows = chunk_s(b, (vps + 1 - k + RING) % RING)
        return rc(G.at[rows], G.at[rows], fw_s.at[b, k], fw_r.at[b, k], SIB)

    def give(sem, dev):
        pl.semaphore_signal(sem, inc=1, device_id=dev, device_id_type=MESH)

    outs = []

    def put(src, dst):
        c = pltpu.make_async_copy(src, dst, out_sem.at[len(outs)])
        c.start()
        outs.append(c)

    def gblk(r, n, c0=0, c1=None):
        return G.at[pl.ds(r, n), pl.ds(c0, (D if c1 is None else c1) - c0)]

    def write_out(b):
        if b < 2:
            put(gblk(b * SUB, SUB), o_wd.at[pl.ds(b * SUB, SUB)])
        elif b < 4:
            put(gblk(b * SUB, SUB), o_wu.at[:, pl.ds((b - 2) * D, D)])
        elif b == 4:
            put(gblk(4 * SUB, L), o_wo)
            put(gblk(4 * SUB + L, L, 0, L), o_wq.at[pl.ds(0, L)])
            put(gblk(4 * SUB + L, L, L, 2 * L), o_wk.at[pl.ds(0, L)])
        else:
            put(gblk(5 * SUB, L, 0, L), o_wq.at[pl.ds(L, L)])
            put(gblk(5 * SUB, L, L, 2 * L), o_wk.at[pl.ds(L, L)])
            put(gblk(5 * SUB + L, L, 0, L), o_wv.at[pl.ds(0, L)])
            put(gblk(5 * SUB + L, L, L, 2 * L), o_wv.at[pl.ds(L, L)])

    def event(b, e):
        if e == 0:
            sib_copy(b).start()
        elif e == 1:
            sib_copy(b).wait_recv()
            G[chunk(b, vp), :] = mine(b, vp)
            rs_copy(b, 0).start()
            sib_copy(b).wait_send()
            give(free_sib.at[b], SIB)
        elif e < RING:
            k = e - 1
            rs_copy(b, k - 1).wait_recv()
            R[b, k - 1] += mine(b, (vp - k + RING) % RING)
            rs_copy(b, k).start()
            if k == 1:
                rs_copy(b, 0).wait_send()
                give(free_ring.at[b], PRV)
        elif e == RING:
            rs_copy(b, RING - 2).wait_recv()
            j = (vp + 1) % RING
            G[chunk(b, j), :] = R[b, RING - 2] + mine(b, j)
            pl.semaphore_wait(free_ring.at[b], 1)
            ag_copy(b, 0).start()
            pl.semaphore_wait(free_sib.at[b], 1)
            fw_copy(b, 0).start()
        elif e < 2 * RING:
            k = e - RING
            ag_in(b, k - 1).wait_recv()
            if k < RING - 1:
                ag_copy(b, k).start()
            fw_copy(b, k).start()
        else:
            for k in range(RING - 1):
                if k:
                    rs_copy(b, k).wait_send()
                ag_copy(b, k).wait_send()
            for k in range(RING):
                fw_copy(b, k).wait_send()
                fw_in(b, k).wait_recv()
            write_out(b)

    progress = {}
    turn = [0]

    def start_batch(b):
        event(b, 0)
        progress[b] = 1

    def pump(n):
        for _ in range(n):
            live = sorted(b for b in progress if progress[b] <= 2 * RING)
            if not live:
                return
            b = live[turn[0] % len(live)]
            turn[0] += 1
            event(b, progress[b])
            progress[b] += 1

    def dwd(rb, _):
        cols = pl.ds(pl.multiple_of(rb * 256, 256), 256)
        G[cols, :] = tn(act[:, cols], db[...])
        return 0

    per = SUB // 256
    lax.fori_loop(0, per, dwd, 0)
    start_batch(0)
    lax.fori_loop(per, 2 * per, dwd, 0)
    start_batch(1)
    pump(1)
    put(hid, o_hid)

    for i in range(NPC):
        y_piece(br, Y_BR, i).wait_send()

    def ffn_back(qc):
        rows = pl.ds(qc * CH, CH)
        bs[rows, :] = jnp.zeros((CH, D), f32)

        def body(fb, _):
            cols = pl.ds(pl.multiple_of(fb * FB, FB), FB)
            low = (nt(db[rows, :], wd_v[cols, :]) * gp[rows, cols].astype(f32)).astype(bf16)
            du[rows, cols] = low
            bs[rows, :] += nt(low, wu_v[:, cols])
            return 0

        lax.fori_loop(0, F // FB, body, 0)

    for qc in range(2):
        ffn_back(qc)
        for i in range(2 * qc, 2 * qc + 2):
            y_piece(fr, Y_FP, i).start()
        pump(2)

    def dwu(base_row):
        def body(cb, _):
            cols = pl.ds(pl.multiple_of(cb * 256, 256), 256)
            fcols = pl.ds(pl.multiple_of(base_row - 2 * SUB + cb * 256, 256), 256)
            G[base_row : base_row + SUB, cols] = tn(fl[...], du[:, fcols])
            return 0

        return body

    lax.fori_loop(0, D // 256, dwu(2 * SUB), 0)
    start_batch(2)
    pump(2)
    lax.fori_loop(0, D // 256, dwu(3 * SUB), 0)
    start_batch(3)
    pump(2)
    for h in range(F // D):
        sm[0, G_UB0 + h : G_UB0 + h + 1, :] = colsum(du[:, h * D : (h + 1) * D].astype(f32))

    pump(6)

    def norm_back(i, _):
        rows = pl.ds(pl.multiple_of(i * PC, PC), PC)
        y_piece(fr, Y_FP, i).wait_recv()
        dfirst = hc[rows, :] + (bs[rows, :] + fr[rows, :])
        xv = xh[rows, :]
        sm[0, G_G1 : G_G1 + 1, :] += colsum(dfirst * xv)
        sm[0, G_S1 : G_S1 + 1, :] += colsum(dfirst)
        dx = dfirst * vec[V_G1 : V_G1 + 1, :]
        dr = rs[rows, 0:1] * (dx - rowmean(dx) - xv * rowmean(dx * xv))
        hc[rows, :] = dr
        low = dr.astype(bf16)
        db[rows, :] = low
        sm[0, G_OB : G_OB + 1, :] += colsum(low.astype(f32))
        return 0

    for i in range(NPC):
        norm_back(i, 0)
        pump(4 if i < NPC - 1 else 1)

    dc = nt(db[...], wo_v[...])
    for par in range(2):
        one = jnp.where(odd == par, dc, 0.0).astype(bf16)
        dcz[par * T : (par + 1) * T, :] = one
        dcTz[par * L : (par + 1) * L, :] = one.T
    pump(1)

    def attend_back(hp, _):
        blk = pl.ds(pl.multiple_of(hp * 128, 128), 128)
        for par in range(2):
            qrows = pl.ds(pl.multiple_of(par * L + hp * 128, 128), 128)
            head = pl.ds(pl.multiple_of(hp * 128 + par * HEAD_DIM, HEAD_DIM), HEAD_DIM)
            for qc in range(2):
                pcols = pl.ds(par * T + qc * CH, CH)
                dp = nn(vn[:, blk], dcTz[qrows, qc * CH : (qc + 1) * CH])
                p = pm[hp, :, pcols].astype(f32)
                t = dp * p
                dsb[:, pcols] = (t - p * colsum(t)).astype(bf16)
            d = nn(kT[head, :], dsb[:, par * T : (par + 1) * T]) * (HEAD_DIM**-0.5)
            dqT[head, :] = d.astype(bf16)
        dk[:, blk] = nn(dsb[...], qz[:, blk]).astype(bf16)
        dv[:, blk] = nn(pm[hp], dcz[:, blk]).astype(bf16)
        return 0

    for hp in range(NP):
        attend_back(hp, 0)
        pump(2)
    dq[...] = dqT[...].T

    for i in range(NPC):
        y_piece(fr, Y_FP, i).wait_send()
    for qc in range(2):
        rows = pl.ds(qc * CH, CH)
        bs[rows, :] = nt(dq[rows, :], wq_v[...]) + nt(dk[rows, :], wk_v[...]) + nt(dv[rows, :], wv_v[...])
        for i in range(2 * qc, 2 * qc + 2):
            y_piece(br, Y_TP, i).start()
    pump(1)
    G[4 * SUB : 4 * SUB + L, :] = nn(ctxT[...], db[...])
    G[4 * SUB + L : 4 * SUB + L + D, 0:L] = tn(tok_v[...], dq[...])
    G[4 * SUB + L : 4 * SUB + L + D, L : 2 * L] = tn(tok_v[...], dk[...])
    start_batch(4)
    pump(2)
    g = tn(tok_v[...], dv[...])
    G[5 * SUB + L : 6 * SUB, 0:L] = g[0:L]
    G[5 * SUB + L : 6 * SUB, L : 2 * L] = g[L : 2 * L]
    start_batch(5)
    pump(2)

    sm[0, G_QV : G_QV + 1, 0:L] = colsum(dq[...].astype(f32))
    sm[0, G_QV : G_QV + 1, L : 2 * L] = colsum(dv[...].astype(f32))

    def sm_copy(k):
        return rc(sm.at[k], smr.at[k], sm_s.at[k], sm_r.at[k], (SIB, XN, Z1, Z2)[k])

    for k in range(4):
        sm_copy(k).start()
        pump(3)
        sm_copy(k).wait()
        sm[k + 1] = sm[k] + smr[k]
    put(sm.at[4], o_sm)
    o_term[...] = trm[...].T[0:1, :]

    for i in range(NPC):
        pump(4)
        rows = pl.ds(i * PC, PC)
        y_piece(br, Y_TP, i).wait_recv()
        hc[rows, :] += bs[rows, :] + br[rows, :]
        put(piece(hc, i), piece(o_tok, i))
    pump(BATCHES * 2 * RING)
    for i in range(NPC):
        y_piece(br, Y_TP, i).wait_send()
    for c in outs:
        c.wait()


def per_device(
    tokens, segment_ids, pad_flags, query_weight, query_bias, key_weight, value_weight, value_bias, output_weight,
    output_bias, first_gain, first_shift, up_weight, up_bias, down_weight, down_bias, second_gain, second_shift,
    term_weight, term_bias, hidden_cot, term_cot, *, groups,
):
    T, D = tokens.shape
    L, F = query_weight.shape[1], up_weight.shape[1]
    vec = jnp.concatenate(
        [query_bias, value_bias, output_bias, first_gain, first_shift, down_bias, second_gain, second_shift, term_weight,
         jnp.broadcast_to(term_bias, (D,))]
    ).astype(f32).reshape(9, D)
    anywhere, vmem = pl.BlockSpec(memory_space=pl.ANY), pl.BlockSpec(memory_space=pltpu.VMEM)
    sub = 3 * F // BATCHES
    dma = pltpu.SemaphoreType.DMA
    V = pltpu.VMEM
    outs = pl.pallas_call(
        kernel,
        out_shape=[
            jax.ShapeDtypeStruct((T, D), bf16),
            jax.ShapeDtypeStruct((1, T), f32),
            jax.ShapeDtypeStruct((T, D), f32),
            jax.ShapeDtypeStruct((D, L), f32),
            jax.ShapeDtypeStruct((D, L), f32),
            jax.ShapeDtypeStruct((D, L), f32),
            jax.ShapeDtypeStruct((L, D), f32),
            jax.ShapeDtypeStruct((D, F), f32),
            jax.ShapeDtypeStruct((F, D), f32),
            jax.ShapeDtypeStruct((16, D), f32),
        ],
        in_specs=[anywhere] + [vmem] * 5 + [anywhere] * 7,
        out_specs=[anywhere, vmem] + [anywhere] * 8,
        scratch_shapes=[
            V((T, D), bf16), V((D, L), bf16), V((D, L), bf16), V((D, L), bf16), V((L, D), bf16), V((L, D), bf16),
            V((D, F), bf16), V((F, D), bf16), V((T, D), f32),
            V((T, L), bf16), V((T, L), bf16), V((L, T), bf16), V((L, T), bf16),
            V((2 * T, L), bf16), V((2 * L, T), bf16), V((L // 128, T, 2 * T), bf16), V((L, T), bf16),
            V((T, D), f32), V((T, 128), f32), V((T, D), bf16),
            V((T, F), bf16), V((T, F), bf16), V((T, D), f32), V((T, D), f32), V((T, D), f32),
            V((T, D), bf16), V((T, F), bf16),
            V((2 * T, L), bf16), V((2 * L, T), bf16), V((T, 2 * T), bf16), V((L, T), bf16),
            V((T, L), bf16), V((T, L), bf16), V((T, L), bf16), V((T, D), bf16), V((T, 8), f32), V((T, 8), f32),
            V((5, 16, D), f32), V((4, 16, D), f32),
            V((3 * F, D), f32), V((BATCHES, sub // 2, D), f32), V((BATCHES, RING - 1, sub // 2 // RING, D), f32),
            dma((8,)), dma((20,)), dma((15,)), dma((15,)), dma((1,)), dma((1,)), dma((2,)), dma((2,)), dma((4,)), dma((4,)),
            dma((BATCHES,)), dma((BATCHES,)), dma((BATCHES, RING - 1)), dma((BATCHES, RING - 1)),
            dma((BATCHES, RING - 1)), dma((BATCHES, RING - 1)), dma((BATCHES, RING)), dma((BATCHES, RING)),
            pltpu.SemaphoreType.REGULAR((BATCHES,)), pltpu.SemaphoreType.REGULAR((BATCHES,)),
        ],
        compiler_params=pltpu.CompilerParams(
            collective_id=0, has_side_effects=True, vmem_limit_bytes=64 * 2**20 - 2**18
        ),
    )(
        tokens, segment_ids, pad_flags, term_cot.reshape(1, T), vec, up_bias.astype(f32).reshape(1, F), query_weight,
        key_weight, value_weight, output_weight, up_weight, down_weight, hidden_cot,
    )
    hidden, term, tokens_grad, gq, gk, gv, go, gu, gd, sm = outs
    if groups > 1:
        gq, gk, gv, go, gu, gd, sm = lax.psum(
            tuple(v * (1.0 / GROUP) for v in (gq, gk, gv, go, gu, gd, sm)), "dp"
        )
    return (
        hidden, term.reshape(T), tokens_grad, gq, sm[G_QV, 0:L], gk, gv, sm[G_QV, L:], go, sm[G_OB], sm[G_G1], sm[G_S1],
        gu, sm[G_UB0 : G_UB1 + 1].reshape(F), gd, sm[G_DB], sm[G_G2], sm[G_S2], sm[G_TW], sm[G_TB, 0:1],
    )


def solution(mesh):
    rows, cols, vec = P("dp", None), P(None, "mp"), P("mp")
    return jax.shard_map(
        partial(per_device, groups=mesh.shape["dp"] // GROUP),
        mesh=mesh,
        in_specs=(
            rows, rows, rows, cols, vec, cols, cols, vec, P("mp", None), P(), P(), P(), cols, vec, P("mp", None), P(), P(),
            P(), P(), P(), rows, P("dp"),
        ),
        out_specs=(
            rows, P("dp"), rows, cols, vec, cols, cols, vec, P("mp", None), P(), P(), P(), cols, vec, P("mp", None), P(),
            P(), P(), P(), P(),
        ),
        check_vma=False,
    )
```

time: 570 us -> 268 us (0.47)
  waiting for transfers between devices: 386 us -> 0 us
  Pallas kernels: 0 us -> 234 us
  blocking collectives: 62.5 us -> 0 us
  matrix products: 48.4 us -> 0 us
  other arithmetic: 29.5 us -> 0.01 us
  between operations: 15.2 us -> 1.36 us
  local copies, waits for them, and re-layouts: 25.9 us -> 31.7 us
    psum x5 -> x0, waiting for transfers between devices: 386 us -> none  [the longest x1 236 us: per_device(): lax.psum((queryweight_grad, querybias_grad, keyweight_grad, valueweight_g...]
    pallas_call x0 -> x1, Pallas kernels: none -> 234 us  [per_device(): pl.pallas_call(kernel, out_shape=[jax.ShapeDtypeStruct((T, D), bf16), jax...]
    psum x1 -> x0, blocking collectives: 62.5 us -> none  [per_device(): lax.psum((queryweight_grad, querybias_grad, keyweight_grad, valueweight_g...]
    dot_general x24 -> x0, matrix products: 48.4 us -> none  [the longest x1 9.34 us: per_device(): jnp.dot(first_low, up_weight, preferred_element_type=jnp.float32)]
    reduce_sum x13 -> x0, other arithmetic: 16.3 us -> none  [the longest x2 5.93 us: layer_norm(): return center * lax.rsqrt(spread + EPS) * gain + shift]
    convert_element_type x11 -> x0, other arithmetic: 7.21 us -> none  [the longest x1 1.86 us: attend_backward(): dscores = (probs * (dprobs - inner)).astype(jnp.bfloat16)]
    unnamed x170 -> x36, local copies, waits for them, and re-layouts: 25.8 us -> 24.2 us
  transfers between devices with their start and end apart: 5 -> 0, of which waited for: 4 -> 0; matrix products, arithmetic and copies ran while one was open for 4% -> 0% of each run, Pallas kernels for 0% -> 0%
where the time goes in v1:
time: 268 us; the launch traced here: 267 us
  Pallas kernels  234 us (87%)
  local copies, waits for them, and re-layouts  31.7 us (12%)
    pallas_call x1, Pallas kernels, per_device(): pl.pallas_call(kernel, out_shape=[jax.ShapeDtypeStruct((T, D), bf16), jax...  234 us
    unnamed x36, local copies, waits for them, and re-layouts  24.2 us

profile of v1, /device:TPU:0, one launch (start us, length us, event | category | flops | bytes accessed | tf_op | source)
XLA Modules:
  0.0 267.4 jit_solution(3061017177881859527)
XLA Ops:
  1.3 1.3 reshape.65.ubv
  2.6 0.9 dynamic-update-slice
  3.5 0.9 dynamic-update-slice.1
  4.3 0.8 dynamic-update-slice.2
  5.2 0.9 dynamic-update-slice.3
  6.0 0.9 dynamic-update-slice.4
  6.9 0.9 dynamic-update-slice.5
  7.7 0.8 dynamic-update-slice.6
  8.6 0.9 dynamic-update-slice.7
  9.4 0.9 dynamic-update-slice.8
  10.9 234.4 %shard_map.365 = (bf16[512,768]{1,0:T(8,128)(2,1)}, f32[1,512]{1,0:T(1,128)}, f32[512,768]{1,0:T(8,128)}, f32[768,384]{1,0:T(8,128)}, f32[768,384]{1,0:T(8,128)}...) custom-call(bf16[512,768]{1,0:T(8,128)(2,1)} %tokens.1, ...), custom_call_target="tpu_custom_call" | custom-call | tf_op jit(solution)/shard_map/pallas_call | solution.py:576
  245.3 1.3 slice.43
  246.6 1.3 slice_reduce_fusion.7
  248.0 0.7 slice.38
  248.7 1.6 slice_reduce_fusion
  250.9 2.2 copy.62
  253.7 1.1 copy.64
  254.9 2.4 copy.65
  257.3 1.0 copy.66
  259.0 1.0 copy.67
  260.7 1.0 copy.68
  261.7 2.4 copy.69
  264.1 0.8 slice-done
  265.2 2.2 copy.70
  (24 shorter events, 3.6 us)
Async XLA Ops:
  245.3 7.8 %copy-start.4 = (f32[1,512]{1,0:T(1,128)S(1)}, f32[1,512]{1,0:T(1,128)}, u32[]{:S(2)}) copy-start(f32[1,512]{1,0:T(1,128)} %get-tuple-element.31) | copy-start | bytes 6148
  245.3 8.4 %copy-start = (f32[512,768]{1,0:T(8,128)S(1)}, f32[512,768]{1,0:T(8,128)}, u32[]{:S(2)}) copy-start(f32[512,768]{1,0:T(8,128)} %get-tuple-element.71) | copy-start | bytes 4718596
  250.9 10.8 %slice-start.2 = ((s8[4718592]{0:T(1024)(128)(4,1)}), s8[4194304]{0:T(1024)(128)(4,1)S(1)}, s32[]{:S(2)}) async-start(s8[4718592]{0:T(1024)(128)(4,1)} %bitcast.7), calls=%async_computation.2 | async-start | bytes 8388608
  253.7 3.6 %copy-start.3 = (f32[768,384]{1,0:T(8,128)S(1)}, f32[768,384]{1,0:T(8,128)}, u32[]{:S(2)}) copy-start(f32[768,384]{1,0:T(8,128)} %get-tuple-element.74) | copy-start | bytes 3538948
  254.9 6.8 %slice-start.3 = ((s8[4718592]{0:T(1024)(128)(4,1)}), s8[524288]{0:T(1024)(128)(4,1)S(1)}, s32[]{:S(2)}) async-start(s8[4718592]{0:T(1024)(128)(4,1)} %bitcast.7), calls=%async_computation.3 | async-start | bytes 1048576
  257.3 1.7 copy-start.2
  259.0 1.7 copy-start.1
  260.7 4.2 %slice-start = ((s8[4718592]{0:T(1024)(128)(4,1)}), s8[4194304]{0:T(1024)(128)(4,1)S(1)}, s32[]{:S(2)}) async-start(s8[4718592]{0:T(1024)(128)(4,1)} %bitcast.5), calls=%async_computation | async-start | bytes 8388608
  261.7 3.5 %slice-start.1 = ((s8[4718592]{0:T(1024)(128)(4,1)}), s8[524288]{0:T(1024)(128)(4,1)S(1)}, s32[]{:S(2)}) async-start(s8[4718592]{0:T(1024)(128)(4,1)} %bitcast.5), calls=%async_computation.1 | async-start | bytes 1048576

commit v2 on v1

--- a/solution.py
+++ b/solution.py
@@ -13,6 +13,7 @@
 RING = 8
 BATCHES = 6
 MESH = pl.DeviceIdType.MESH
+VMEM_LIMIT = 47 * 2**20
 bf16, f32 = jnp.bfloat16, jnp.float32
 
 V_QV, V_OB, V_G1, V_S1, V_DB, V_G2, V_S2, V_TW, V_TB = range(9)
@@ -40,12 +41,13 @@
 
 
 def kernel(
-    tokens, seg, pad, tcot, vec, ubv, wq, wk, wv, wo, wu, wd, hcot,
-    o_hid, o_term, o_tok, o_wq, o_wk, o_wv, o_wo, o_wu, o_wd, o_sm,
-    tok_v, wq_v, wk_v, wv_v, wo_v, woo_v, wu_v, wd_v, hc,
+    tokens, seg, pad, tcot, i_qb, i_vb, i_ob, i_g1, i_s1, i_ub, i_db, i_g2, i_s2, i_tw, i_tb, wq, wk, wv, wo, wu, wd, hcot,
+    G, hc, hid, o_term, smt,
+    v_tcot, v_qb, v_vb, v_ob, v_g1, v_s1, v_ub, v_db, v_g2, v_s2, v_tw, vec, ubv,
+    tok_v, wq_v, wk_v, wv_v, wo_v, woo_v, wu_v, wd_v,
     kn, vn, kT, vT, qz, qTz, pm, ctxT, xh, rs, fl, gp, act, bs, br, fr, db, du,
-    dcz, dcTz, dsb, dqT, dq, dk, dv, hid, col, trm, sm, smr, G, S, R,
-    ld_sem, out_sem, y_s, y_r, wx_s, wx_r, ws_s, ws_r, sm_s, sm_r,
+    dcz, dcTz, dsb, dqT, dq, dk, dv, col, trm, sm, smr, S, R,
+    ld_sem, y_s, y_r, wx_s, wx_r, ws_s, ws_r, sm_s, sm_r,
     sib_s, sib_r, rs_s, rs_r, ag_s, ag_r, fw_s, fw_r, free_sib, free_ring,
 ):
     T, D = tokens.shape
@@ -86,11 +88,13 @@
 
     pairs = [
         (tokens, tok_v), (wq, wq_v), (wk, wk_v), (wv, wv_v), (wo, wo_v), (wu, wu_v), (wd, wd_v), (hcot, hc),
+        (tcot, v_tcot), (i_qb, v_qb), (i_vb, v_vb), (i_ob, v_ob), (i_g1, v_g1), (i_s1, v_s1), (i_ub, v_ub), (i_db, v_db),
+        (i_g2, v_g2), (i_s2, v_s2), (i_tw, v_tw),
     ]
     loads = [pltpu.make_async_copy(a, b, ld_sem.at[i]) for i, (a, b) in enumerate(pairs)]
     for c in loads:
         c.start()
-    L_TOK, L_WQ, L_WK, L_WV, L_WO, L_WU, L_WD, L_HC = loads
+    L_TOK, L_WQ, L_WK, L_WV, L_WO, L_WU, L_WD, L_HC, *L_VEC = loads
 
     peers = (YN, SIB, NXT, PRV, XN, Z1, Z2)
     bar = pltpu.get_barrier_semaphore()
@@ -128,6 +132,20 @@
         rc(wor(share_s), wor(share_s), ws_s.at[0], ws_r.at[0], SIB),
         rc(wor(share_sx), wor(share_sx), ws_s.at[1], ws_r.at[1], SIB),
     ]
+
+    for c in L_VEC:
+        c.wait()
+    vec[V_QV : V_QV + 1, 0:L] = v_qb[...].astype(f32).reshape(1, L)
+    vec[V_QV : V_QV + 1, L : 2 * L] = v_vb[...].astype(f32).reshape(1, L)
+    vec[V_OB : V_OB + 1, :] = v_ob[...].astype(f32).reshape(1, D)
+    vec[V_G1 : V_G1 + 1, :] = v_g1[...].astype(f32).reshape(1, D)
+    vec[V_S1 : V_S1 + 1, :] = v_s1[...].astype(f32).reshape(1, D)
+    vec[V_DB : V_DB + 1, :] = v_db[...].astype(f32).reshape(1, D)
+    vec[V_G2 : V_G2 + 1, :] = v_g2[...].astype(f32).reshape(1, D)
+    vec[V_S2 : V_S2 + 1, :] = v_s2[...].astype(f32).reshape(1, D)
+    vec[V_TW : V_TW + 1, :] = v_tw[...].astype(f32).reshape(1, D)
+    vec[V_TB : V_TB + 1, :] = jnp.broadcast_to(i_tb[...].astype(f32).reshape(1, 1), (1, D))
+    ubv[...] = v_ub[...].astype(f32).reshape(1, F)
 
     L_TOK.wait()
     L_WQ.wait()
@@ -148,7 +166,7 @@
     vT[...] = vv.T
 
     segf, padf = seg[...].astype(f32), pad[...].astype(f32)
-    rows8 = jnp.concatenate([segf, padf, tcot[...], jnp.zeros((5, T), f32)], axis=0)
+    rows8 = jnp.concatenate([segf, padf, v_tcot[...].reshape(1, T), jnp.zeros((5, T), f32)], axis=0)
     col[...] = rows8.T
     for qc in range(2):
         ki = lax.broadcasted_iota(jnp.int32, (T, CH), 0)
@@ -325,31 +343,6 @@
 
     def give(sem, dev):
         pl.semaphore_signal(sem, inc=1, device_id=dev, device_id_type=MESH)
-
-    outs = []
-
-    def put(src, dst):
-        c = pltpu.make_async_copy(src, dst, out_sem.at[len(outs)])
-        c.start()
-        outs.append(c)
-
-    def gblk(r, n, c0=0, c1=None):
-        return G.at[pl.ds(r, n), pl.ds(c0, (D if c1 is None else c1) - c0)]
-
-    def write_out(b):
-        if b < 2:
-            put(gblk(b * SUB, SUB), o_wd.at[pl.ds(b * SUB, SUB)])
-        elif b < 4:
-            put(gblk(b * SUB, SUB), o_wu.at[:, pl.ds((b - 2) * D, D)])
-        elif b == 4:
-            put(gblk(4 * SUB, L), o_wo)
-            put(gblk(4 * SUB + L, L, 0, L), o_wq.at[pl.ds(0, L)])
-            put(gblk(4 * SUB + L, L, L, 2 * L), o_wk.at[pl.ds(0, L)])
-        else:
-            put(gblk(5 * SUB, L, 0, L), o_wq.at[pl.ds(L, L)])
-            put(gblk(5 * SUB, L, L, 2 * L), o_wk.at[pl.ds(L, L)])
-            put(gblk(5 * SUB + L, L, 0, L), o_wv.at[pl.ds(0, L)])
-            put(gblk(5 * SUB + L, L, L, 2 * L), o_wv.at[pl.ds(L, L)])
 
     def event(b, e):
         if e == 0:
@@ -390,7 +383,6 @@
             for k in range(RING):
                 fw_copy(b, k).wait_send()
                 fw_in(b, k).wait_recv()
-            write_out(b)
 
     progress = {}
     turn = [0]
@@ -420,7 +412,6 @@
     lax.fori_loop(per, 2 * per, dwd, 0)
     start_batch(1)
     pump(1)
-    put(hid, o_hid)
 
     for i in range(NPC):
         y_piece(br, Y_BR, i).wait_send()
@@ -541,20 +532,58 @@
         sm_copy(k).start()
         pump(3)
         sm_copy(k).wait()
-        sm[k + 1] = sm[k] + smr[k]
-    put(sm.at[4], o_sm)
-    o_term[...] = trm[...].T[0:1, :]
+        if k < 3:
+            sm[k + 1] = sm[k] + smr[k]
+        else:
+            smt[...] = sm[k] + smr[k]
+    o_term[...] = trm[...].T
 
     for i in range(NPC):
         pump(4)
         rows = pl.ds(i * PC, PC)
         y_piece(br, Y_TP, i).wait_recv()
         hc[rows, :] += bs[rows, :] + br[rows, :]
-        put(piece(hc, i), piece(o_tok, i))
     pump(BATCHES * 2 * RING)
     for i in range(NPC):
         y_piece(br, Y_TP, i).wait_send()
-    for c in outs:
+
+
+def spread(
+    G, hc, hid, term, smt,
+    o_hid, o_term, o_tok, o_wq, o_qb, o_wk, o_wv, o_vb, o_wo, o_ob, o_g1, o_s1, o_wu, o_ub, o_wd, o_db, o_g2, o_s2, o_tw,
+    o_tb,
+    sem,
+):
+    D, L = o_wq.shape
+    F = o_wu.shape[1]
+    SUB = G.shape[0] // BATCHES
+
+    def g(r, n, c0=0, c1=D):
+        return G.at[pl.ds(r, n), pl.ds(c0, c1 - c0)]
+
+    q = 4 * SUB + L
+    copies = [(g(0, F), o_wd)]
+    copies += [(g(F + h * D, D), o_wu.at[:, pl.ds(h * D, D)]) for h in range(F // D)]
+    copies += [
+        (hc, o_tok), (hid, o_hid), (g(4 * SUB, L), o_wo), (g(q, D, 0, L), o_wq), (g(q, D, L, 2 * L), o_wk),
+        (g(q + D, L, 0, L), o_wv.at[pl.ds(0, L)]), (g(q + D, L, L, 2 * L), o_wv.at[pl.ds(L, L)]),
+    ]
+    started = [pltpu.make_async_copy(a, b, sem.at[i]) for i, (a, b) in enumerate(copies)]
+    for c in started:
+        c.start()
+    o_term[...] = term[0, :]
+    o_qb[...] = smt[G_QV, 0:L]
+    o_vb[...] = smt[G_QV, L : 2 * L]
+    o_ob[...] = smt[G_OB, :]
+    o_g1[...] = smt[G_G1, :]
+    o_s1[...] = smt[G_S1, :]
+    o_ub[...] = jnp.concatenate([smt[G_UB0 + h : G_UB0 + h + 1, :] for h in range(F // D)], axis=1).reshape(F)
+    o_db[...] = smt[G_DB, :]
+    o_g2[...] = smt[G_G2, :]
+    o_s2[...] = smt[G_S2, :]
+    o_tw[...] = smt[G_TW, :]
+    o_tb[...] = smt[G_TB : G_TB + 1, 0:1].reshape(1)
+    for c in started:
         c.wait()
 
 
@@ -565,63 +594,63 @@
 ):
     T, D = tokens.shape
     L, F = query_weight.shape[1], up_weight.shape[1]
-    vec = jnp.concatenate(
-        [query_bias, value_bias, output_bias, first_gain, first_shift, down_bias, second_gain, second_shift, term_weight,
-         jnp.broadcast_to(term_bias, (D,))]
-    ).astype(f32).reshape(9, D)
     anywhere, vmem = pl.BlockSpec(memory_space=pl.ANY), pl.BlockSpec(memory_space=pltpu.VMEM)
     sub = 3 * F // BATCHES
     dma = pltpu.SemaphoreType.DMA
     V = pltpu.VMEM
-    outs = pl.pallas_call(
+    G, hc, hid, term, smt = pl.pallas_call(
         kernel,
-        out_shape=[
-            jax.ShapeDtypeStruct((T, D), bf16),
-            jax.ShapeDtypeStruct((1, T), f32),
-            jax.ShapeDtypeStruct((T, D), f32),
-            jax.ShapeDtypeStruct((D, L), f32),
-            jax.ShapeDtypeStruct((D, L), f32),
-            jax.ShapeDtypeStruct((D, L), f32),
-            jax.ShapeDtypeStruct((L, D), f32),
-            jax.ShapeDtypeStruct((D, F), f32),
-            jax.ShapeDtypeStruct((F, D), f32),
-            jax.ShapeDtypeStruct((16, D), f32),
-        ],
-        in_specs=[anywhere] + [vmem] * 5 + [anywhere] * 7,
-        out_specs=[anywhere, vmem] + [anywhere] * 8,
+        out_shape=[V((3 * F, D), f32), V((T, D), f32), V((T, D), bf16), V((8, T), f32), V((16, D), f32)],
+        in_specs=[anywhere, vmem, vmem] + [anywhere] * 11 + [vmem] + [anywhere] * 7,
+        out_specs=[vmem] * 5,
         scratch_shapes=[
+            V((T,), f32), V((L,), bf16), V((L,), bf16), V((D,), bf16), V((D,), bf16), V((D,), bf16), V((F,), bf16),
+            V((D,), bf16), V((D,), bf16), V((D,), bf16), V((D,), bf16), V((16, D), f32), V((1, F), f32),
             V((T, D), bf16), V((D, L), bf16), V((D, L), bf16), V((D, L), bf16), V((L, D), bf16), V((L, D), bf16),
-            V((D, F), bf16), V((F, D), bf16), V((T, D), f32),
+            V((D, F), bf16), V((F, D), bf16),
             V((T, L), bf16), V((T, L), bf16), V((L, T), bf16), V((L, T), bf16),
             V((2 * T, L), bf16), V((2 * L, T), bf16), V((L // 128, T, 2 * T), bf16), V((L, T), bf16),
             V((T, D), f32), V((T, 128), f32), V((T, D), bf16),
             V((T, F), bf16), V((T, F), bf16), V((T, D), f32), V((T, D), f32), V((T, D), f32),
             V((T, D), bf16), V((T, F), bf16),
             V((2 * T, L), bf16), V((2 * L, T), bf16), V((T, 2 * T), bf16), V((L, T), bf16),
-            V((T, L), bf16), V((T, L), bf16), V((T, L), bf16), V((T, D), bf16), V((T, 8), f32), V((T, 8), f32),
-            V((5, 16, D), f32), V((4, 16, D), f32),
-            V((3 * F, D), f32), V((BATCHES, sub // 2, D), f32), V((BATCHES, RING - 1, sub // 2 // RING, D), f32),
-            dma((8,)), dma((20,)), dma((15,)), dma((15,)), dma((1,)), dma((1,)), dma((2,)), dma((2,)), dma((4,)), dma((4,)),
+            V((T, L), bf16), V((T, L), bf16), V((T, L), bf16), V((T, 8), f32), V((T, 8), f32),
+            V((4, 16, D), f32), V((4, 16, D), f32),
+            V((BATCHES, sub // 2, D), f32), V((BATCHES, RING - 1, sub // 2 // RING, D), f32),
+            dma((19,)), dma((15,)), dma((15,)), dma((1,)), dma((1,)), dma((2,)), dma((2,)), dma((4,)), dma((4,)),
             dma((BATCHES,)), dma((BATCHES,)), dma((BATCHES, RING - 1)), dma((BATCHES, RING - 1)),
             dma((BATCHES, RING - 1)), dma((BATCHES, RING - 1)), dma((BATCHES, RING)), dma((BATCHES, RING)),
             pltpu.SemaphoreType.REGULAR((BATCHES,)), pltpu.SemaphoreType.REGULAR((BATCHES,)),
         ],
         compiler_params=pltpu.CompilerParams(
-            collective_id=0, has_side_effects=True, vmem_limit_bytes=64 * 2**20 - 2**18
+            collective_id=0, has_side_effects=True, vmem_limit_bytes=VMEM_LIMIT
         ),
     )(
-        tokens, segment_ids, pad_flags, term_cot.reshape(1, T), vec, up_bias.astype(f32).reshape(1, F), query_weight,
-        key_weight, value_weight, output_weight, up_weight, down_weight, hidden_cot,
+        tokens, segment_ids, pad_flags, term_cot, query_bias, value_bias, output_bias, first_gain, first_shift, up_bias,
+        down_bias, second_gain, second_shift, term_weight, term_bias, query_weight, key_weight, value_weight,
+        output_weight, up_weight, down_weight, hidden_cot,
     )
-    hidden, term, tokens_grad, gq, gk, gv, go, gu, gd, sm = outs
+    vector = [jax.ShapeDtypeStruct((n,), f32) for n in (D, L, F, T, 1)]
+    vd, vl, vf, vt, v1 = vector
+    dl = jax.ShapeDtypeStruct((D, L), f32)
+    outs = pl.pallas_call(
+        spread,
+        out_shape=[
+            jax.ShapeDtypeStruct((T, D), bf16), vt, jax.ShapeDtypeStruct((T, D), f32), dl, vl, dl, dl, vl,
+            jax.ShapeDtypeStruct((L, D), f32), vd, vd, vd, jax.ShapeDtypeStruct((D, F), f32), vf,
+            jax.ShapeDtypeStruct((F, D), f32), vd, vd, vd, vd, v1,
+        ],
+        in_specs=[vmem] * 5,
+        out_specs=[
+            anywhere, vmem, anywhere, anywhere, vmem, anywhere, anywhere, vmem, anywhere, vmem, vmem, vmem, anywhere, vmem,
+            anywhere, vmem, vmem, vmem, vmem, vmem,
+        ],
+        scratch_shapes=[dma((16,))],
+        compiler_params=pltpu.CompilerParams(vmem_limit_bytes=2**20),
+    )(G, hc, hid, term, smt)
     if groups > 1:
-        gq, gk, gv, go, gu, gd, sm = lax.psum(
-            tuple(v * (1.0 / GROUP) for v in (gq, gk, gv, go, gu, gd, sm)), "dp"
-        )
-    return (
-        hidden, term.reshape(T), tokens_grad, gq, sm[G_QV, 0:L], gk, gv, sm[G_QV, L:], go, sm[G_OB], sm[G_G1], sm[G_S1],
-        gu, sm[G_UB0 : G_UB1 + 1].reshape(F), gd, sm[G_DB], sm[G_G2], sm[G_S2], sm[G_TW], sm[G_TB, 0:1],
-    )
+        outs = list(outs[:3]) + list(lax.psum(tuple(v * (1.0 / GROUP) for v in outs[3:]), "dp"))
+    return tuple(outs)
 
 
 def solution(mesh):

time: 268 us -> 241 us (0.90)
  local copies, waits for them, and re-layouts: 31.7 us -> 0 us
  Pallas kernels: 234 us -> 240 us
    unnamed x36 -> x0, local copies, waits for them, and re-layouts: 24.2 us -> none
    pallas_call x1 -> x2, Pallas kernels: 234 us -> 240 us  [the longest x1 233 us: per_device(): pl.pallas_call(kernel, out_shape=[V((3 * F, D), f32), V((T, D), f32), V((...]
    slice x4 -> x0, local copies, waits for them, and re-layouts: 4.97 us -> none  [the longest x1 1.6 us: per_device(): sm[G_TW]]
where the time goes in v2:
time: 241 us
  Pallas kernels  240 us (100%)
    pallas_call x1, Pallas kernels, per_device(): pl.pallas_call(kernel, out_shape=[V((3 * F, D), f32), V((T, D), f32), V((...  233 us
    pallas_call x1, Pallas kernels, per_device(): pl.pallas_call(spread, out_shape=[jax.ShapeDtypeStruct((T, D), bf16), vt,...  6.53 us

profile of v2, /device:TPU:0, one launch (start us, length us, event | category | flops | bytes accessed | tf_op | source)
XLA Modules:
  0.0 241.2 jit_solution(9626150591090657154)
XLA Ops:
  1.3 233.2 %shard_map.365 = (f32[4608,768]{1,0:T(8,128)S(1)}, f32[512,768]{1,0:T(8,128)S(1)}, bf16[512,768]{1,0:T(8,128)(2,1)S(1)}, f32[8,512]{1,0:T(8,128)S(1)}, f32[16,768]{1,0:T(8,128)S(1)}) custom-call(bf16[512,768]{1,0:T(8,128)(2,1)} %tokens.1, s32[1,512]{1,0:T(1,128)} %seg.1, s32[1,512]{1,0:T(1,128)} %pad.1, f32[512]{0:T(512)} %tcot.1, bf16[384]{0:T(512)(128)(2,1)} %i_qb.1, ...), custom_call_target="tpu_custom_call" | custom-call | tf_op jit(solution)/shard_map/pallas_call | solution.py:601
  234.5 6.5 %shard_map.366 = (bf16[512,768]{1,0:T(8,128)(2,1)}, f32[512]{0:T(512)}, f32[512,768]{1,0:T(8,128)}, f32[768,384]{1,0:T(8,128)}, f32[384]{0:T(512)}, /*index=5*/f...) custom-call(f32[4608,768]{1,0:T(8,128)S(1)} %get-tuple-element.25.G,, ...), custom_call_target="tpu_custom_call" | custom-call | tf_op jit(solution)/shard_map/pallas_call | solution.py:636

commit v3 on v2

--- a/solution.py
+++ b/solution.py
@@ -1,3 +1,4 @@
+from collections import deque
 from functools import partial
 
 import jax
@@ -11,7 +12,7 @@
 EPS = 1e-06
 GROUP = 16
 RING = 8
-BATCHES = 6
+BATCHES = 12
 MESH = pl.DeviceIdType.MESH
 VMEM_LIMIT = 47 * 2**20
 bf16, f32 = jnp.bfloat16, jnp.float32
@@ -375,43 +376,34 @@
             if k < RING - 1:
                 ag_copy(b, k).start()
             fw_copy(b, k).start()
-        else:
-            for k in range(RING - 1):
-                if k:
-                    rs_copy(b, k).wait_send()
-                ag_copy(b, k).wait_send()
-            for k in range(RING):
-                fw_copy(b, k).wait_send()
-                fw_in(b, k).wait_recv()
-
-    progress = {}
-    turn = [0]
+
+    def finish(b):
+        for k in range(RING - 1):
+            if k:
+                rs_copy(b, k).wait_send()
+            ag_copy(b, k).wait_send()
+        for k in range(RING):
+            fw_copy(b, k).wait_send()
+            fw_in(b, k).wait_recv()
+
+    queue = deque()
 
     def start_batch(b):
         event(b, 0)
-        progress[b] = 1
+        queue.append((b, 1))
 
     def pump(n):
         for _ in range(n):
-            live = sorted(b for b in progress if progress[b] <= 2 * RING)
-            if not live:
+            if not queue:
                 return
-            b = live[turn[0] % len(live)]
-            turn[0] += 1
-            event(b, progress[b])
-            progress[b] += 1
-
-    def dwd(rb, _):
-        cols = pl.ds(pl.multiple_of(rb * 256, 256), 256)
-        G[cols, :] = tn(act[:, cols], db[...])
-        return 0
-
-    per = SUB // 256
-    lax.fori_loop(0, per, dwd, 0)
-    start_batch(0)
-    lax.fori_loop(per, 2 * per, dwd, 0)
-    start_batch(1)
-    pump(1)
+            b, e = queue.popleft()
+            event(b, e)
+            if e + 1 < 2 * RING:
+                queue.append((b, e + 1))
+
+    for b in range(4):
+        G[b * SUB : (b + 1) * SUB, :] = tn(act[:, b * SUB : (b + 1) * SUB], db[...])
+        start_batch(b)
 
     for i in range(NPC):
         y_piece(br, Y_BR, i).wait_send()
@@ -435,25 +427,15 @@
             y_piece(fr, Y_FP, i).start()
         pump(2)
 
-    def dwu(base_row):
-        def body(cb, _):
-            cols = pl.ds(pl.multiple_of(cb * 256, 256), 256)
-            fcols = pl.ds(pl.multiple_of(base_row - 2 * SUB + cb * 256, 256), 256)
-            G[base_row : base_row + SUB, cols] = tn(fl[...], du[:, fcols])
-            return 0
-
-        return body
-
-    lax.fori_loop(0, D // 256, dwu(2 * SUB), 0)
-    start_batch(2)
-    pump(2)
-    lax.fori_loop(0, D // 256, dwu(3 * SUB), 0)
-    start_batch(3)
-    pump(2)
+    for b in range(4):
+        rows, cols = b % 2 * SUB, b // 2 * D
+        G[(4 + b) * SUB : (5 + b) * SUB, :] = tn(fl[:, rows : rows + SUB], du[:, cols : cols + D])
+        start_batch(4 + b)
+        pump(2)
     for h in range(F // D):
         sm[0, G_UB0 + h : G_UB0 + h + 1, :] = colsum(du[:, h * D : (h + 1) * D].astype(f32))
 
-    pump(6)
+    pump(7)
 
     def norm_back(i, _):
         rows = pl.ds(pl.multiple_of(i * PC, PC), PC)
@@ -472,7 +454,7 @@
 
     for i in range(NPC):
         norm_back(i, 0)
-        pump(4 if i < NPC - 1 else 1)
+        pump(11 if i < NPC - 1 else 1)
 
     dc = nt(db[...], wo_v[...])
     for par in range(2):
@@ -500,7 +482,7 @@
 
     for hp in range(NP):
         attend_back(hp, 0)
-        pump(2)
+        pump(3)
     dq[...] = dqT[...].T
 
     for i in range(NPC):
@@ -510,16 +492,18 @@
         bs[rows, :] = nt(dq[rows, :], wq_v[...]) + nt(dk[rows, :], wk_v[...]) + nt(dv[rows, :], wv_v[...])
         for i in range(2 * qc, 2 * qc + 2):
             y_piece(br, Y_TP, i).start()
-    pump(1)
-    G[4 * SUB : 4 * SUB + L, :] = nn(ctxT[...], db[...])
-    G[4 * SUB + L : 4 * SUB + L + D, 0:L] = tn(tok_v[...], dq[...])
-    G[4 * SUB + L : 4 * SUB + L + D, L : 2 * L] = tn(tok_v[...], dk[...])
-    start_batch(4)
     pump(2)
-    g = tn(tok_v[...], dv[...])
-    G[5 * SUB + L : 6 * SUB, 0:L] = g[0:L]
-    G[5 * SUB + L : 6 * SUB, L : 2 * L] = g[L : 2 * L]
-    start_batch(5)
+    G[8 * SUB : 9 * SUB, :] = nn(ctxT[...], db[...])
+    start_batch(8)
+    for b in range(2):
+        half = pl.ds(b * SUB, SUB)
+        G[(9 + b) * SUB : (10 + b) * SUB, 0:L] = tn(tok_v[:, half], dq[...])
+        G[(9 + b) * SUB : (10 + b) * SUB, L : 2 * L] = tn(tok_v[:, half], dk[...])
+        start_batch(9 + b)
+        pump(2)
+    for b in range(2):
+        G[11 * SUB : 12 * SUB, b * L : (b + 1) * L] = tn(tok_v[:, b * SUB : (b + 1) * SUB], dv[...])
+    start_batch(11)
     pump(2)
 
     sm[0, G_QV : G_QV + 1, 0:L] = colsum(dq[...].astype(f32))
@@ -530,7 +514,7 @@
 
     for k in range(4):
         sm_copy(k).start()
-        pump(3)
+        pump(4)
         sm_copy(k).wait()
         if k < 3:
             sm[k + 1] = sm[k] + smr[k]
@@ -539,11 +523,13 @@
     o_term[...] = trm[...].T
 
     for i in range(NPC):
-        pump(4)
+        pump(10)
         rows = pl.ds(i * PC, PC)
         y_piece(br, Y_TP, i).wait_recv()
         hc[rows, :] += bs[rows, :] + br[rows, :]
     pump(BATCHES * 2 * RING)
+    for b in range(BATCHES):
+        finish(b)
     for i in range(NPC):
         y_piece(br, Y_TP, i).wait_send()
 
@@ -556,16 +542,15 @@
 ):
     D, L = o_wq.shape
     F = o_wu.shape[1]
-    SUB = G.shape[0] // BATCHES
 
     def g(r, n, c0=0, c1=D):
         return G.at[pl.ds(r, n), pl.ds(c0, c1 - c0)]
 
-    q = 4 * SUB + L
+    q = 2 * F + L
     copies = [(g(0, F), o_wd)]
     copies += [(g(F + h * D, D), o_wu.at[:, pl.ds(h * D, D)]) for h in range(F // D)]
     copies += [
-        (hc, o_tok), (hid, o_hid), (g(4 * SUB, L), o_wo), (g(q, D, 0, L), o_wq), (g(q, D, L, 2 * L), o_wk),
+        (hc, o_tok), (hid, o_hid), (g(2 * F, L), o_wo), (g(q, D, 0, L), o_wq), (g(q, D, L, 2 * L), o_wk),
         (g(q + D, L, 0, L), o_wv.at[pl.ds(0, L)]), (g(q + D, L, L, 2 * L), o_wv.at[pl.ds(L, L)]),
     ]
     started = [pltpu.make_async_copy(a, b, sem.at[i]) for i, (a, b) in enumerate(copies)]

time: 241 us -> 225 us (0.934)
  Pallas kernels: 240 us -> 224 us
    pallas_call x1, Pallas kernels: 233 us -> 217 us  [per_device(): pl.pallas_call(kernel, out_shape=[V((3 * F, D), f32), V((T, D), f32), V((...]
where the time goes in v3:
time: 225 us
  Pallas kernels  224 us (100%)
    pallas_call x1, Pallas kernels, per_device(): pl.pallas_call(kernel, out_shape=[V((3 * F, D), f32), V((T, D), f32), V((...  217 us
    pallas_call x1, Pallas kernels, per_device(): pl.pallas_call(spread, out_shape=[jax.ShapeDtypeStruct((T, D), bf16), vt,...  6.53 us

profile of v3, /device:TPU:0, one launch (start us, length us, event | category | flops | bytes accessed | tf_op | source)
XLA Modules:
  0.0 225.1 jit_solution(4474656968349237929)
XLA Ops:
  1.3 217.1 %shard_map.365 = (f32[4608,768]{1,0:T(8,128)S(1)}, f32[512,768]{1,0:T(8,128)S(1)}, bf16[512,768]{1,0:T(8,128)(2,1)S(1)}, f32[8,512]{1,0:T(8,128)S(1)}, f32[16,768]{1,0:T(8,128)S(1)}) custom-call(bf16[512,768]{1,0:T(8,128)(2,1)} %tokens.1, s32[1,512]{1,0:T(1,128)} %seg.1, s32[1,512]{1,0:T(1,128)} %pad.1, f32[512]{0:T(512)} %tcot.1, bf16[384]{0:T(512)(128)(2,1)} %i_qb.1, ...), custom_call_target="tpu_custom_call" | custom-call | tf_op jit(solution)/shard_map/pallas_call | solution.py:586
  218.4 6.5 %shard_map.366 = (bf16[512,768]{1,0:T(8,128)(2,1)}, f32[512]{0:T(512)}, f32[512,768]{1,0:T(8,128)}, f32[768,384]{1,0:T(8,128)}, f32[384]{0:T(512)}, /*index=5*/f...) custom-call(f32[4608,768]{1,0:T(8,128)S(1)} %get-tuple-element.25.G,, ...), custom_call_target="tpu_custom_call" | custom-call | tf_op jit(solution)/shard_map/pallas_call | solution.py:621

commit v4 on v3

v4 whole, which is shorter than its diff:
```python
from collections import deque
from functools import partial

import jax
import jax.numpy as jnp
from jax import lax
from jax.experimental import pallas as pl
from jax.experimental.pallas import tpu as pltpu
from jax.sharding import PartitionSpec as P

HEAD_DIM = 64
EPS = 1e-06
GROUP = 16
RING = 8
BATCHES = 12
MESH = pl.DeviceIdType.MESH
PUMPS = (2, 2, 5, 10, 3, 2, 4, 10)
VMEM_LIMIT = 47 * 2**20
bf16, f32 = jnp.bfloat16, jnp.float32

V_QV, V_OB, V_G1, V_S1, V_DB, V_G2, V_S2, V_TW, V_TB = range(9)
G_QV, G_OB, G_G1, G_S1, G_UB0, G_UB1, G_DB, G_G2, G_S2, G_TW, G_TB = range(11)


def nn(a, b):
    return jnp.dot(a, b, preferred_element_type=f32)


def nt(a, b):
    return lax.dot_general(a, b, (((1,), (1,)), ((), ())), preferred_element_type=f32)


def tn(a, b):
    return lax.dot_general(a, b, (((0,), (0,)), ((), ())), preferred_element_type=f32)


def colsum(v):
    return jnp.sum(v, axis=0, keepdims=True)


def rowmean(v):
    return jnp.mean(v, axis=-1, keepdims=True)


def kernel(
    tokens, i_seg, i_pad, tcot, i_qb, i_vb, i_ob, i_g1, i_s1, i_ub, i_db, i_g2, i_s2, i_tw, i_tb, wq, wk, wv, wo, wu, wd, hcot,
    G, hc, hid, o_term, smt,
    v_tcot, v_qb, v_vb, v_ob, v_g1, v_s1, v_ub, v_db, v_g2, v_s2, v_tw, v_tb, seg, pad, vec, ubv,
    tok_v, wq_v, wk_v, wv_v, wo_v, woo_v, wu_v, wd_v,
    kn, vn, kT, vT, qz, qTz, pm, ctxT, xh, rs, first_v, fl, gp, act, bs, br, fr, db, du,
    dcz, dcTz, dqT, col, trm, sm, smr, S, R,
    ld_sem, y_s, y_r, wo_s, wo_r, sm_s, sm_r, sib_s, sib_r, ring_s, ring_r, fw_s, fw_r, free_sib,
):
    T, D = tokens.shape
    L, F = wq.shape[1], wu.shape[1]
    NP = L // 128
    CH, PC, FB = T // 2, T // 4, 512
    NPC = T // PC
    SUB = G.shape[0] // BATCHES
    HALF, CK = SUB // 2, SUB // 2 // RING

    me, mp = lax.axis_index("dp"), lax.axis_index("mp")
    base, rank = me // GROUP * GROUP, me % GROUP
    core, chip = rank % 2, rank // 2
    x, z = chip % 2, chip // 2
    pos = jnp.where(x == 0, z, RING - 1 - z)
    vp = jnp.where(core == 0, pos, (RING - pos) % RING)

    def at_vp(v):
        p = jnp.where(core == 0, v, (RING - v) % RING)
        c = jnp.where(p < RING // 2, 2 * p, 2 * (RING - 1 - p) + 1)
        return (base + 2 * c + core, mp)

    def at_xz(ax, az):
        return (base + 2 * (2 * az + ax) + core, mp)

    YN = (me, 1 - mp)
    SIB = (base + 2 * chip + 1 - core, mp)
    NXT, PRV = at_vp((vp + 1) % RING), at_vp((vp + RING - 1) % RING)
    XN = at_xz(1 - x, z)
    Z1 = at_xz(x, z // 2 * 2 + 1 - z % 2)
    Z2 = at_xz(x, (z + 2) % 4)

    def rc(src, dst, ss, rr, dev):
        return pltpu.make_async_remote_copy(
            src_ref=src, dst_ref=dst, send_sem=ss, recv_sem=rr, device_id=dev, device_id_type=MESH
        )

    pairs = [
        (wo, wo_v), (tokens, tok_v), (wq, wq_v), (wk, wk_v), (wv, wv_v), (wu, wu_v), (wd, wd_v), (hcot, hc),
        (tcot, v_tcot), (i_qb, v_qb), (i_vb, v_vb), (i_ob, v_ob), (i_g1, v_g1), (i_s1, v_s1), (i_ub, v_ub), (i_db, v_db),
        (i_g2, v_g2), (i_s2, v_s2), (i_tw, v_tw), (i_tb, v_tb), (i_seg, seg), (i_pad, pad),
    ]
    loads = [pltpu.make_async_copy(a, b, ld_sem.at[i]) for i, (a, b) in enumerate(pairs)]
    for c in loads:
        c.start()
    L_WO, L_TOK, L_WQ, L_WK, L_WV, L_WU, L_WD, L_HC, *L_VEC = loads

    peers = (YN, SIB, NXT, PRV, XN, Z1, Z2)
    bar = pltpu.get_barrier_semaphore()
    for d in peers:
        pl.semaphore_signal(bar, inc=1, device_id=d, device_id_type=MESH)
    pl.semaphore_wait(bar, len(peers))

    r_wor = 4 * SUB
    r_wos = r_wor + L
    r_bias = 8 * SUB
    r_cs = r_bias + T
    r_cr = r_cs + L
    SH = L // 8

    def wor(ax, az, ac):
        return G.at[pl.ds(pl.multiple_of(r_wor + ((az * 2 + ax) * 2 + ac) * SH, 16), SH)]

    zp = z % 2
    L_WO.wait()
    G[r_wos : r_wos + SH, :] = wo_v[pl.ds(pl.multiple_of(((zp * 2 + x) * 2 + core) * SH, 16), SH), :].astype(f32)

    def wo_copy(k):
        ax, az = ((x, zp), (x, zp), (x, zp), (1 - x, zp), (x, zp), (1 - x, zp), (x, 1 - zp), (1 - x, 1 - zp))[k]
        place = wor(ax, az, core)
        if k == 0:
            return rc(G.at[pl.ds(r_wos, SH)], place, y_s.at[0], y_r.at[0], YN)
        return rc(place, place, wo_s, wo_r.at[min(k, 4) - 1], (XN, Z1, Z1, SIB, SIB, SIB, SIB)[k - 1])

    wo_copy(0).start()

    for c in L_VEC:
        c.wait()
    vec[V_QV : V_QV + 1, 0:L] = v_qb[...].astype(f32).reshape(1, L)
    vec[V_QV : V_QV + 1, L : 2 * L] = v_vb[...].astype(f32).reshape(1, L)
    vec[V_OB : V_OB + 1, :] = v_ob[...].astype(f32).reshape(1, D)
    vec[V_G1 : V_G1 + 1, :] = v_g1[...].astype(f32).reshape(1, D)
    vec[V_S1 : V_S1 + 1, :] = v_s1[...].astype(f32).reshape(1, D)
    vec[V_DB : V_DB + 1, :] = v_db[...].astype(f32).reshape(1, D)
    vec[V_G2 : V_G2 + 1, :] = v_g2[...].astype(f32).reshape(1, D)
    vec[V_S2 : V_S2 + 1, :] = v_s2[...].astype(f32).reshape(1, D)
    vec[V_TW : V_TW + 1, :] = v_tw[...].astype(f32).reshape(1, D)
    vec[V_TB : V_TB + 1, :] = jnp.broadcast_to(v_tb[...].astype(f32).reshape(1, 1), (1, D))
    ubv[...] = v_ub[...].astype(f32).reshape(1, F)

    L_TOK.wait()
    L_WQ.wait()
    lane = lax.broadcasted_iota(jnp.int32, (T, L), 1)
    odd = (lane // HEAD_DIM) % 2
    qv = (nn(tok_v[...], wq_v[...]) + vec[V_QV : V_QV + 1, 0:L]).astype(bf16).astype(f32) * (HEAD_DIM**-0.5)
    for par in range(2):
        one = jnp.where(odd == par, qv, 0.0).astype(bf16)
        qz[par * T : (par + 1) * T, :] = one
        qTz[par * L : (par + 1) * L, :] = one.T
    L_WK.wait()
    kv = nn(tok_v[...], wk_v[...]).astype(bf16)
    kn[...] = kv
    kT[...] = kv.T
    L_WV.wait()
    vv = (nn(tok_v[...], wv_v[...]) + vec[V_QV : V_QV + 1, L : 2 * L]).astype(bf16)
    vn[...] = vv
    vT[...] = vv.T

    segf, padf = seg[...].astype(f32), pad[...].astype(f32)
    rows8 = jnp.concatenate([segf, padf, v_tcot[...].reshape(1, T), jnp.zeros((5, T), f32)], axis=0)
    col[...] = rows8.T
    for qc in range(T // CH):
        ki = lax.broadcasted_iota(jnp.int32, (T, CH), 0)
        qi = lax.broadcasted_iota(jnp.int32, (T, CH), 1) + qc * CH
        same = col[:, 0:1] == segf[:, qc * CH : (qc + 1) * CH]
        allowed = same & ((col[:, 1:2] == 0.0) | (ki == qi))
        G[r_bias : r_bias + T, qc * CH : (qc + 1) * CH] = jnp.where(allowed, 0.0, -1e9)

    Y_CTX, Y_BR, Y_FP, Y_TP = 1, 1 + NPC, 1 + 2 * NPC, 1 + 3 * NPC

    def span(i):
        return pl.ds(pl.multiple_of(i * PC, PC), PC)

    def ctx_copy(i):
        return rc(G.at[pl.ds(r_cs, L), span(i)], G.at[pl.ds(r_cr, L), span(i)], y_s.at[1], y_r.at[Y_CTX + i], YN)

    def attend(i):
        def body(hp, _):
            blk = pl.ds(pl.multiple_of(hp * 128, 128), 128)
            for par in range(2):
                qrows = pl.ds(pl.multiple_of(par * L + hp * 128, 128), 128)
                head = pl.multiple_of(hp * 128 + par * HEAD_DIM, HEAD_DIM)
                s = nn(kn[:, blk], qTz[qrows, span(i)]) + G[r_bias : r_bias + T, span(i)]
                e = jnp.exp(s - jnp.max(s, axis=0, keepdims=True))
                p = (e * (1.0 / colsum(e))).astype(bf16)
                pm[hp, :, pl.ds(par * T + i * PC, PC)] = p
                c = nn(vT[pl.ds(head, HEAD_DIM), :], p).astype(bf16)
                ctxT[pl.ds(head, HEAD_DIM), span(i)] = c
                G[pl.ds(pl.multiple_of(r_cs + head, HEAD_DIM), HEAD_DIM), span(i)] = c.astype(f32)
            return 0

        lax.fori_loop(0, NP, body, 0)

    for i in range(NPC):
        attend(i)
        ctx_copy(i).start()
        if i == 1:
            wo_copy(0).wait_recv()
            for k in (1, 2, 4):
                wo_copy(k).start()
        if i == 3:
            wo_copy(1).wait_recv()
            for k in (3, 5):
                wo_copy(k).start()
    for k in (2, 3):
        wo_copy(k).wait_recv()
        wo_copy(k + 4).start()

    def piece(buf, i):
        return buf.at[span(i)]

    def y_piece(dst, which, i):
        return rc(piece(bs, i), piece(dst, i), y_s.at[which - 3 + i], y_r.at[which + i], YN)

    def y_sent(dst, which):
        for i in range(NPC):
            y_piece(dst, which, i).wait_send()

    L_WU.wait()
    L_WD.wait()
    some = G.at[pl.ds(r_wor, 4 * SH)]
    rc(some, some, wo_s, wo_r.at[3], SIB).wait_recv()
    woo_v[...] = G[r_wor : r_wor + L, :].astype(bf16)

    def forward(i, _):
        rows = span(i)
        ctx_copy(i).wait_recv()
        other = G[r_cr : r_cr + L, rows].astype(bf16)
        res = tok_v[rows, :].astype(f32) + (tn(ctxT[:, rows], wo_v[...]) + tn(other, woo_v[...])) + vec[V_OB : V_OB + 1, :]
        cen = res - rowmean(res)
        rstd = lax.rsqrt(rowmean(cen * cen) + EPS)
        xv = cen * rstd
        xh[rows, :] = xv
        rs[rows, :] = jnp.broadcast_to(rstd, (PC, 128))
        first = xv * vec[V_G1 : V_G1 + 1, :] + vec[V_S1 : V_S1 + 1, :]
        first_v[rows, :] = first
        fl[rows, :] = first.astype(bf16)
        bs[rows, :] = jnp.zeros((PC, D), f32)

        def body(fb, _):
            cols = pl.ds(pl.multiple_of(fb * FB, FB), FB)
            u = nn(fl[rows, :], wu_v[:, cols]) + ubv[:, cols]
            ph = 0.5 + 0.5 * lax.erf(u * 0.7071067811865476)
            a = (u * ph).astype(bf16)
            act[rows, cols] = a
            gp[rows, cols] = (ph + u * (jnp.exp(-0.5 * u * u) * 0.3989422804014327)).astype(bf16)
            bs[rows, :] += nn(a, wd_v[cols, :])
            return 0

        lax.fori_loop(0, F // FB, body, 0)
        y_piece(br, Y_BR, i).start()
        return 0

    lax.fori_loop(0, NPC, forward, 0)
    wo_copy(0).wait_send()
    some = G.at[pl.ds(r_wor, 7 * SH)]
    rc(some, some, wo_s, wo_r.at[3], SIB).wait_send()
    rc(G.at[pl.ds(r_cs, L), pl.ds(0, T)], G.at[pl.ds(r_cr, L), pl.ds(0, T)], y_s.at[1], y_r.at[Y_CTX], YN).wait_send()

    sm[0] = jnp.zeros((16, D), f32)
    L_HC.wait()

    def tail(i):
        rows = span(i)
        y_piece(br, Y_BR, i).wait_recv()
        first = first_v[rows, :]
        res = first + (bs[rows, :] + br[rows, :]) + vec[V_DB : V_DB + 1, :]
        cen = res - rowmean(res)
        rstd = lax.rsqrt(rowmean(cen * cen) + EPS)
        xv = cen * rstd
        g2 = vec[V_G2 : V_G2 + 1, :]
        tw = vec[V_TW : V_TW + 1, :]
        second = xv * g2 + vec[V_S2 : V_S2 + 1, :]
        hid[rows, :] = second.astype(bf16)
        v = jnp.sum(second * tw, axis=-1, keepdims=True) + vec[V_TB : V_TB + 1, 0:1]
        keep = 1.0 - col[rows, 1:2]
        soft = jnp.maximum(v, 0.0) + jnp.log1p(jnp.exp(-jnp.abs(v)))
        trm[rows, :] = jnp.broadcast_to(soft * keep, (PC, 8))
        dterm = col[rows, 2:3] * keep * lax.logistic(v)
        dsec = hc[rows, :] + dterm * tw
        sm[0, G_G2 : G_G2 + 1, :] += colsum(dsec * xv)
        sm[0, G_S2 : G_S2 + 1, :] += colsum(dsec)
        sm[0, G_TW : G_TW + 1, :] += colsum(dterm * second)
        sm[0, G_TB : G_TB + 1, :] += jnp.broadcast_to(colsum(dterm), (1, D))
        dx = dsec * g2
        dr = rstd * (dx - rowmean(dx) - xv * rowmean(dx * xv))
        hc[rows, :] = dr
        low = dr.astype(bf16)
        db[rows, :] = low
        sm[0, G_DB : G_DB + 1, :] += colsum(low.astype(f32))

    def ffn_back(i, between):
        rows = span(i)
        y_piece(br, Y_BR, i).wait_send()
        for fb in range(F // FB):
            cols = pl.ds(fb * FB, FB)
            low = (nt(db[rows, :], wd_v[cols, :]) * gp[rows, cols].astype(f32)).astype(bf16)
            du[rows, cols] = low
            part = nt(low, wu_v[:, cols])
            if fb == 0:
                bs[rows, :] = part
            else:
                bs[rows, :] += part
            between()
        y_piece(fr, Y_FP, i).start()

    def tail_back(i, _):
        tail(i)
        ffn_back(i, lambda: None)
        return 0

    early = (NPC - 1) * PC

    def down_grad(b, part):
        return tn(act[part, b * SUB : (b + 1) * SUB], db[part, :])

    def up_grad(b, part):
        rows, cols = b % 2 * SUB, b // 2 * D
        return tn(fl[part, rows : rows + SUB], du[part, cols : cols + D])

    lax.fori_loop(0, NPC - 1, tail_back, 0)
    for b in range(4):
        G[b * SUB : (b + 1) * SUB, :] = down_grad(b, pl.ds(0, early))
    for b in range(4):
        G[(4 + b) * SUB : (5 + b) * SUB, :] = up_grad(b, pl.ds(0, early))
    tail(NPC - 1)

    def chunk(b, j):
        return pl.ds(pl.multiple_of(b * SUB + core * HALF + j * CK, 8), CK)

    def own(b, j):
        return S.at[b, pl.ds(pl.multiple_of(j * CK, 8), CK)]

    def mine(b, j):
        return G[chunk(b, j), :] + own(b, j)[...]

    def sib_copy(b):
        src = G.at[pl.ds(pl.multiple_of(b * SUB + (1 - core) * HALF, 8), HALF)]
        return rc(src, S.at[b], sib_s.at[b], sib_r.at[b], SIB)

    def rs_copy(b, k):
        src = own(b, vp) if k == 0 else R.at[b, k - 1]
        return rc(src, R.at[b, k], ring_s, ring_r.at[b, k], NXT)

    def ag_copy(b, k, back):
        rows = G.at[chunk(b, (vp + 1 - back - k + RING) % RING)]
        return rc(rows, rows, ring_s, ring_r.at[b, k - 1 if k else RING - 1], NXT)

    def fw_copy(b, k):
        rows = G.at[chunk(b, (vp + 1 - k + RING) % RING)]
        return rc(rows, rows, fw_s, fw_r, SIB)

    def event(b, e):
        if e == 0:
            sib_copy(b).start()
        elif e == 1:
            sib_copy(b).wait_recv()
            own(b, vp)[...] += G[chunk(b, vp), :]
            rs_copy(b, 0).start()
            sib_copy(b).wait_send()
            pl.semaphore_signal(free_sib.at[b], inc=1, device_id=SIB, device_id_type=MESH)
        elif e < RING:
            k = e - 1
            rs_copy(b, k - 1).wait_recv()
            R[b, k - 1] += mine(b, (vp - k + RING) % RING)
            rs_copy(b, k).start()
        elif e == RING:
            rs_copy(b, RING - 2).wait_recv()
            j = (vp + 1) % RING
            G[chunk(b, j), :] = R[b, RING - 2] + mine(b, j)
            ag_copy(b, 0, 0).start()
            pl.semaphore_wait(free_sib.at[b], 1)
            fw_copy(b, 0).start()
        else:
            k = e - RING
            ag_copy(b, k - 1, 1).wait_recv()
            if k < RING - 1:
                ag_copy(b, k, 0).start()
            fw_copy(b, k).start()

    def finish():
        sent = G.at[pl.ds(0, BATCHES * 2 * (RING - 1) * CK)]
        rc(sent, sent, ring_s, ring_r.at[0, 0], NXT).wait_send()
        half = G.at[pl.ds(0, BATCHES * HALF)]
        rc(half, half, fw_s, fw_r, SIB).wait()

    queue = deque()

    def start_batch(b):
        event(b, 0)
        queue.append((b, 1))

    def pump(n):
        for _ in range(n):
            if not queue:
                return
            b, e = queue.popleft()
            event(b, e)
            if e + 1 < 2 * RING:
                queue.append((b, e + 1))

    last = pl.ds(early, PC)
    for b in range(4):
        G[b * SUB : (b + 1) * SUB, :] += down_grad(b, last)
        start_batch(b)
    ffn_back(NPC - 1, lambda: pump(PUMPS[0]))
    for b in range(4):
        G[(4 + b) * SUB : (5 + b) * SUB, :] += up_grad(b, last)
        start_batch(4 + b)
        pump(PUMPS[1])
    for h in range(F // D):
        sm[0, G_UB0 + h : G_UB0 + h + 1, :] = colsum(du[:, h * D : (h + 1) * D].astype(f32))

    pump(PUMPS[2])

    def norm_back(i, _):
        rows = span(i)
        y_piece(fr, Y_FP, i).wait_recv()
        dfirst = hc[rows, :] + (bs[rows, :] + fr[rows, :])
        xv = xh[rows, :]
        sm[0, G_G1 : G_G1 + 1, :] += colsum(dfirst * xv)
        sm[0, G_S1 : G_S1 + 1, :] += colsum(dfirst)
        dx = dfirst * vec[V_G1 : V_G1 + 1, :]
        dr = rs[rows, 0:1] * (dx - rowmean(dx) - xv * rowmean(dx * xv))
        hc[rows, :] = dr
        low = dr.astype(bf16)
        db[rows, :] = low
        sm[0, G_OB : G_OB + 1, :] += colsum(low.astype(f32))
        return 0

    for i in range(NPC):
        norm_back(i, 0)
        pump(PUMPS[3] if i < NPC - 1 else 1)

    dc = nt(db[...], wo_v[...])
    for par in range(2):
        one = jnp.where(odd == par, dc, 0.0).astype(bf16)
        dcz[par * T : (par + 1) * T, :] = one
        dcTz[par * L : (par + 1) * L, :] = one.T
    pump(1)

    dsb = act.at[:, pl.ds(0, 2 * T)]
    dq, dk, dv = (gp.at[:, pl.ds(k * L, L)] for k in range(3))

    def attend_back(hp, _):
        blk = pl.ds(pl.multiple_of(hp * 128, 128), 128)
        for par in range(2):
            qrows = pl.ds(pl.multiple_of(par * L + hp * 128, 128), 128)
            head = pl.ds(pl.multiple_of(hp * 128 + par * HEAD_DIM, HEAD_DIM), HEAD_DIM)
            for qc in range(2):
                pcols = pl.ds(par * T + qc * CH, CH)
                dp = nn(vn[:, blk], dcTz[qrows, qc * CH : (qc + 1) * CH])
                p = pm[hp, :, pcols].astype(f32)
                t = dp * p
                dsb[:, pcols] = (t - p * colsum(t)).astype(bf16)
            d = nn(kT[head, :], dsb[:, par * T : (par + 1) * T]) * (HEAD_DIM**-0.5)
            dqT[head, :] = d.astype(bf16)
        dk[:, blk] = nn(dsb[...], qz[:, blk]).astype(bf16)
        dv[:, blk] = nn(pm[hp], dcz[:, blk]).astype(bf16)
        return 0

    for hp in range(NP):
        attend_back(hp, 0)
        pump(PUMPS[4])
    dq[...] = dqT[...].T

    y_sent(fr, Y_FP)
    for qc in range(2):
        rows = pl.ds(qc * CH, CH)
        bs[rows, :] = nt(dq[rows, :], wq_v[...]) + nt(dk[rows, :], wk_v[...]) + nt(dv[rows, :], wv_v[...])
        for i in range(2 * qc, 2 * qc + 2):
            y_piece(br, Y_TP, i).start()
    pump(PUMPS[5])
    G[8 * SUB : 9 * SUB, :] = nn(ctxT[...], db[...])
    start_batch(8)
    for b in range(2):
        half = pl.ds(b * SUB, SUB)
        G[(9 + b) * SUB : (10 + b) * SUB, 0:L] = tn(tok_v[:, half], dq[...])
        G[(9 + b) * SUB : (10 + b) * SUB, L : 2 * L] = tn(tok_v[:, half], dk[...])
        start_batch(9 + b)
        pump(PUMPS[5])
    for b in range(2):
        G[11 * SUB : 12 * SUB, b * L : (b + 1) * L] = tn(tok_v[:, b * SUB : (b + 1) * SUB], dv[...])
    start_batch(11)
    pump(PUMPS[5])

    sm[0, G_QV : G_QV + 1, 0:L] = colsum(dq[...].astype(f32))
    sm[0, G_QV : G_QV + 1, L : 2 * L] = colsum(dv[...].astype(f32))

    def sm_copy(k):
        return rc(sm.at[k], smr.at[k], sm_s.at[k], sm_r.at[k], (SIB, XN, Z1, Z2)[k])

    for k in range(4):
        sm_copy(k).start()
        pump(PUMPS[6])
        sm_copy(k).wait()
        if k < 3:
            sm[k + 1] = sm[k] + smr[k]
        else:
            smt[...] = sm[k] + smr[k]
    o_term[...] = trm[...].T

    for i in range(NPC):
        pump(PUMPS[7])
        rows = pl.ds(i * PC, PC)
        y_piece(br, Y_TP, i).wait_recv()
        hc[rows, :] += bs[rows, :] + br[rows, :]
    pump(BATCHES * 2 * RING)
    finish()
    y_sent(br, Y_TP)


def spread(
    G, hc, hid, term, smt,
    o_hid, o_term, o_tok, o_wq, o_qb, o_wk, o_wv, o_vb, o_wo, o_ob, o_g1, o_s1, o_wu, o_ub, o_wd, o_db, o_g2, o_s2, o_tw,
    o_tb,
    sem, *small,
):
    D, L = o_wq.shape
    F = o_wu.shape[1]

    def g(r, n, c0=0, c1=D):
        return G.at[pl.ds(r, n), pl.ds(c0, c1 - c0)]

    q = 2 * F + L
    copies = [(g(0, F), o_wd)]
    copies += [(g(F + h * D, D), o_wu.at[:, pl.ds(h * D, D)]) for h in range(F // D)]
    copies += [
        (hc, o_tok), (hid, o_hid), (g(2 * F, L), o_wo), (g(q, D, 0, L), o_wq), (g(q, D, L, 2 * L), o_wk),
        (g(q + D, L, 0, L), o_wv.at[pl.ds(0, L)]), (g(q + D, L, L, 2 * L), o_wv.at[pl.ds(L, L)]),
    ]
    started = [pltpu.make_async_copy(a, b, sem.at[i]) for i, (a, b) in enumerate(copies)]
    for c in started:
        c.start()
    rows = [term[0, :], smt[G_QV, 0:L], smt[G_QV, L : 2 * L]]
    rows += [smt[r, :] for r in (G_OB, G_G1, G_S1, G_DB, G_G2, G_S2, G_TW)]
    rows.append(jnp.concatenate([smt[G_UB0 + h : G_UB0 + h + 1, :] for h in range(F // D)], axis=1).reshape(F))
    rows.append(smt[G_TB : G_TB + 1, 0:1].reshape(1))
    places = (o_term, o_qb, o_vb, o_ob, o_g1, o_s1, o_db, o_g2, o_s2, o_tw, o_ub, o_tb)
    for i, (row, held, place) in enumerate(zip(rows, small, places)):
        held[...] = row
        started.append(pltpu.make_async_copy(held, place, sem.at[len(copies) + i]))
        started[-1].start()
    for c in started:
        c.wait()


def per_device(
    tokens, segment_ids, pad_flags, query_weight, query_bias, key_weight, value_weight, value_bias, output_weight,
    output_bias, first_gain, first_shift, up_weight, up_bias, down_weight, down_bias, second_gain, second_shift,
    term_weight, term_bias, hidden_cot, term_cot, *, groups,
):
    T, D = tokens.shape
    L, F = query_weight.shape[1], up_weight.shape[1]
    anywhere, vmem = pl.BlockSpec(memory_space=pl.ANY), pl.BlockSpec(memory_space=pltpu.VMEM)
    sub = 3 * F // BATCHES
    dma = pltpu.SemaphoreType.DMA
    V = pltpu.VMEM
    G, hc, hid, term, smt = pl.pallas_call(
        kernel,
        out_shape=[V((3 * F, D), f32), V((T, D), f32), V((T, D), bf16), V((8, T), f32), V((16, D), f32)],
        in_specs=[anywhere] * 22,
        out_specs=[vmem] * 5,
        scratch_shapes=[
            V((T,), f32), V((L,), bf16), V((L,), bf16), V((D,), bf16), V((D,), bf16), V((D,), bf16), V((F,), bf16),
            V((D,), bf16), V((D,), bf16), V((D,), bf16), V((D,), bf16), V((1,), bf16), V((1, T), jnp.int32), V((1, T), jnp.int32),
            V((16, D), f32), V((1, F), f32),
            V((T, D), bf16), V((D, L), bf16), V((D, L), bf16), V((D, L), bf16), V((L, D), bf16), V((L, D), bf16),
            V((D, F), bf16), V((F, D), bf16),
            V((T, L), bf16), V((T, L), bf16), V((L, T), bf16), V((L, T), bf16),
            V((2 * T, L), bf16), V((2 * L, T), bf16), V((L // 128, T, 2 * T), bf16), V((L, T), bf16),
            V((T, D), f32), V((T, 128), f32), V((T, D), f32), V((T, D), bf16),
            V((T, F), bf16), V((T, F), bf16), V((T, D), f32), V((T, D), f32), V((T, D), f32),
            V((T, D), bf16), V((T, F), bf16),
            V((2 * T, L), bf16), V((2 * L, T), bf16), V((L, T), bf16),
            V((T, 8), f32), V((T, 8), f32),
            V((4, 16, D), f32), V((4, 16, D), f32),
            V((BATCHES, sub // 2, D), f32), V((BATCHES, RING - 1, sub // 2 // RING, D), f32),
            dma((22,)), dma((14,)), dma((17,)), dma, dma((4,)), dma((4,)), dma((4,)),
            dma((BATCHES,)), dma((BATCHES,)), dma, dma((BATCHES, RING)), dma, dma, pltpu.SemaphoreType.REGULAR((BATCHES,)),
        ],
        compiler_params=pltpu.CompilerParams(
            collective_id=0, has_side_effects=True, vmem_limit_bytes=VMEM_LIMIT
        ),
    )(
        tokens, segment_ids, pad_flags, term_cot, query_bias, value_bias, output_bias, first_gain, first_shift, up_bias,
        down_bias, second_gain, second_shift, term_weight, term_bias, query_weight, key_weight, value_weight,
        output_weight, up_weight, down_weight, hidden_cot,
    )
    vector = [jax.ShapeDtypeStruct((n,), f32) for n in (D, L, F, T, 1)]
    vd, vl, vf, vt, v1 = vector
    dl = jax.ShapeDtypeStruct((D, L), f32)
    outs = pl.pallas_call(
        spread,
        out_shape=[
            jax.ShapeDtypeStruct((T, D), bf16), vt, jax.ShapeDtypeStruct((T, D), f32), dl, vl, dl, dl, vl,
            jax.ShapeDtypeStruct((L, D), f32), vd, vd, vd, jax.ShapeDtypeStruct((D, F), f32), vf,
            jax.ShapeDtypeStruct((F, D), f32), vd, vd, vd, vd, v1,
        ],
        in_specs=[vmem] * 5,
        out_specs=[anywhere] * 20,
        scratch_shapes=[dma((24,)), V((T,), f32), V((L,), f32), V((L,), f32)]
        + [V((D,), f32)] * 7
        + [V((F,), f32), V((1,), f32)],
        compiler_params=pltpu.CompilerParams(vmem_limit_bytes=2**20),
    )(G, hc, hid, term, smt)
    if groups > 1:
        outs = list(outs[:3]) + list(lax.psum(tuple(v * (1.0 / GROUP) for v in outs[3:]), "dp"))
    return tuple(outs)


def solution(mesh):
    rows, cols, vec = P("dp", None), P(None, "mp"), P("mp")
    return jax.shard_map(
        partial(per_device, groups=mesh.shape["dp"] // GROUP),
        mesh=mesh,
        in_specs=(
            rows, rows, rows, cols, vec, cols, cols, vec, P("mp", None), P(), P(), P(), cols, vec, P("mp", None), P(), P(),
            P(), P(), P(), rows, P("dp"),
        ),
        out_specs=(
            rows, P("dp"), rows, cols, vec, cols, cols, vec, P("mp", None), P(), P(), P(), cols, vec, P("mp", None), P(),
            P(), P(), P(), P(),
        ),
        check_vma=False,
    )
```

time: 225 us -> 217 us (0.964)
  Pallas kernels: 224 us -> 215 us
    pallas_call x1, Pallas kernels: 217 us -> 209 us  [per_device(): pl.pallas_call(kernel, out_shape=[V((3 * F, D), f32), V((T, D), f32), V((...]
where the time goes in v4:
time: 217 us
  Pallas kernels  215 us (99%)
    pallas_call x1, Pallas kernels, per_device(): pl.pallas_call(kernel, out_shape=[V((3 * F, D), f32), V((T, D), f32), V((...  209 us
    pallas_call x1, Pallas kernels, per_device(): pl.pallas_call(spread, out_shape=[jax.ShapeDtypeStruct((T, D), bf16), vt,...  5.98 us

profile of v4, /device:TPU:0, one launch (start us, length us, event | category | flops | bytes accessed | tf_op | source)
XLA Modules:
  0.0 216.6 jit_solution(2312967591449900837)
XLA Ops:
  1.3 209.1 %shard_map.365 = (f32[4608,768]{1,0:T(8,128)S(1)}, f32[512,768]{1,0:T(8,128)S(1)}, bf16[512,768]{1,0:T(8,128)(2,1)S(1)}, f32[8,512]{1,0:T(8,128)S(1)}, f32[16,768]{1,0:T(8,128)S(1)}) custom-call(bf16[512,768]{1,0:T(8,128)(2,1)} %tokens.1, s32[1,512]{1,0:T(1,128)} %i_seg.1, s32[1,512]{1,0:T(1,128)} %i_pad.1, f32[512]{0:T(512)} %tcot.1, bf16[384]{0:T(512)(128)(2,1)} %i_qb.1, ...), custom_call_target="tpu_custom_call" | custom-call | tf_op jit(solution)/shard_map/pallas_call | solution.py:560
  210.4 6.0 %shard_map.366 = (bf16[512,768]{1,0:T(8,128)(2,1)}, f32[512]{0:T(512)}, f32[512,768]{1,0:T(8,128)}, f32[768,384]{1,0:T(8,128)}, f32[384]{0:T(512)}, /*index=5*/f...) custom-call(f32[4608,768]{1,0:T(8,128)S(1)} %get-tuple-element.25.G,, ...), custom_call_target="tpu_custom_call" | custom-call | tf_op jit(solution)/shard_map/pallas_call | solution.py:594

commit v5 on v4

--- a/solution.py
+++ b/solution.py
@@ -1,4 +1,3 @@
-from collections import deque
 from functools import partial
 
 import jax
@@ -12,9 +11,9 @@
 EPS = 1e-06
 GROUP = 16
 RING = 8
-BATCHES = 12
 MESH = pl.DeviceIdType.MESH
-PUMPS = (2, 2, 5, 10, 3, 2, 4, 10)
+DOWN, UP, ATTN = [3] * 4, [4] * 3, [4] * 3
+PUMPS = (1, 1, 4, 9, 3, 3, 5, 10)
 VMEM_LIMIT = 47 * 2**20
 bf16, f32 = jnp.bfloat16, jnp.float32
 
@@ -40,6 +39,12 @@
 
 def rowmean(v):
     return jnp.mean(v, axis=-1, keepdims=True)
+
+
+def sub_batches(ff):
+    unit = ff // 12
+    sizes = [n * unit for n in DOWN + UP + ATTN]
+    return [sum(sizes[:b]) for b in range(len(sizes))], sizes
 
 
 def kernel(
@@ -56,8 +61,8 @@
     NP = L // 128
     CH, PC, FB = T // 2, T // 4, 512
     NPC = T // PC
-    SUB = G.shape[0] // BATCHES
-    HALF, CK = SUB // 2, SUB // 2 // RING
+    SUB = L
+    starts, sizes = sub_batches(F)
 
     me, mp = lax.axis_index("dp"), lax.axis_index("mp")
     base, rank = me // GROUP * GROUP, me % GROUP
@@ -327,21 +332,25 @@
     tail(NPC - 1)
 
     def chunk(b, j):
-        return pl.ds(pl.multiple_of(b * SUB + core * HALF + j * CK, 8), CK)
+        return pl.ds(pl.multiple_of(starts[b] + core * (sizes[b] // 2) + j * (sizes[b] // 2 // RING), 8), sizes[b] // 2 // RING)
 
     def own(b, j):
-        return S.at[b, pl.ds(pl.multiple_of(j * CK, 8), CK)]
+        return S.at[pl.ds(pl.multiple_of(starts[b] // 2 + j * (sizes[b] // 2 // RING), 8), sizes[b] // 2 // RING)]
+
+    def slot(b, k):
+        size = sizes[b] // 2 // RING
+        return R.at[pl.ds(starts[b] // 2 // RING * (RING - 1) + k * size, size)]
 
     def mine(b, j):
         return G[chunk(b, j), :] + own(b, j)[...]
 
     def sib_copy(b):
-        src = G.at[pl.ds(pl.multiple_of(b * SUB + (1 - core) * HALF, 8), HALF)]
-        return rc(src, S.at[b], sib_s.at[b], sib_r.at[b], SIB)
+        half = sizes[b] // 2
+        src = G.at[pl.ds(pl.multiple_of(starts[b] + (1 - core) * half, 8), half)]
+        return rc(src, S.at[pl.ds(starts[b] // 2, half)], sib_s.at[b], sib_r.at[b], SIB)
 
     def rs_copy(b, k):
-        src = own(b, vp) if k == 0 else R.at[b, k - 1]
-        return rc(src, R.at[b, k], ring_s, ring_r.at[b, k], NXT)
+        return rc(own(b, vp) if k == 0 else slot(b, k - 1), slot(b, k), ring_s, ring_r.at[b, k], NXT)
 
     def ag_copy(b, k, back):
         rows = G.at[chunk(b, (vp + 1 - back - k + RING) % RING)]
@@ -363,12 +372,12 @@
         elif e < RING:
             k = e - 1
             rs_copy(b, k - 1).wait_recv()
-            R[b, k - 1] += mine(b, (vp - k + RING) % RING)
+            slot(b, k - 1)[...] += mine(b, (vp - k + RING) % RING)
             rs_copy(b, k).start()
         elif e == RING:
             rs_copy(b, RING - 2).wait_recv()
             j = (vp + 1) % RING
-            G[chunk(b, j), :] = R[b, RING - 2] + mine(b, j)
+            G[chunk(b, j), :] = slot(b, RING - 2)[...] + mine(b, j)
             ag_copy(b, 0, 0).start()
             pl.semaphore_wait(free_sib.at[b], 1)
             fw_copy(b, 0).start()
@@ -380,34 +389,41 @@
             fw_copy(b, k).start()
 
     def finish():
-        sent = G.at[pl.ds(0, BATCHES * 2 * (RING - 1) * CK)]
+        sent = G.at[pl.ds(0, 3 * F // RING * (RING - 1))]
         rc(sent, sent, ring_s, ring_r.at[0, 0], NXT).wait_send()
-        half = G.at[pl.ds(0, BATCHES * HALF)]
+        half = G.at[pl.ds(0, 3 * F // 2)]
         rc(half, half, fw_s, fw_r, SIB).wait()
 
-    queue = deque()
-
-    def start_batch(b):
-        event(b, 0)
-        queue.append((b, 1))
+    queue = []
+
+    begun = [0]
+
+    def complete(rows):
+        while begun[0] < len(starts) and starts[begun[0]] + sizes[begun[0]] <= rows:
+            event(begun[0], 0)
+            queue.append((begun[0], 1))
+            begun[0] += 1
 
     def pump(n):
         for _ in range(n):
             if not queue:
                 return
-            b, e = queue.popleft()
+            b, e = queue.pop(0)
             event(b, e)
             if e + 1 < 2 * RING:
-                queue.append((b, e + 1))
+                place = len(queue)
+                while place > 4 and queue[place - 1][1] > e + 1:
+                    place -= 1
+                queue.insert(place, (b, e + 1))
 
     last = pl.ds(early, PC)
     for b in range(4):
         G[b * SUB : (b + 1) * SUB, :] += down_grad(b, last)
-        start_batch(b)
+        complete((b + 1) * SUB)
     ffn_back(NPC - 1, lambda: pump(PUMPS[0]))
     for b in range(4):
         G[(4 + b) * SUB : (5 + b) * SUB, :] += up_grad(b, last)
-        start_batch(4 + b)
+        complete((5 + b) * SUB)
         pump(PUMPS[1])
     for h in range(F // D):
         sm[0, G_UB0 + h : G_UB0 + h + 1, :] = colsum(du[:, h * D : (h + 1) * D].astype(f32))
@@ -473,16 +489,16 @@
             y_piece(br, Y_TP, i).start()
     pump(PUMPS[5])
     G[8 * SUB : 9 * SUB, :] = nn(ctxT[...], db[...])
-    start_batch(8)
+    complete(9 * SUB)
     for b in range(2):
         half = pl.ds(b * SUB, SUB)
         G[(9 + b) * SUB : (10 + b) * SUB, 0:L] = tn(tok_v[:, half], dq[...])
         G[(9 + b) * SUB : (10 + b) * SUB, L : 2 * L] = tn(tok_v[:, half], dk[...])
-        start_batch(9 + b)
+        complete((10 + b) * SUB)
         pump(PUMPS[5])
     for b in range(2):
         G[11 * SUB : 12 * SUB, b * L : (b + 1) * L] = tn(tok_v[:, b * SUB : (b + 1) * SUB], dv[...])
-    start_batch(11)
+    complete(12 * SUB)
     pump(PUMPS[5])
 
     sm[0, G_QV : G_QV + 1, 0:L] = colsum(dq[...].astype(f32))
@@ -506,7 +522,7 @@
         rows = pl.ds(i * PC, PC)
         y_piece(br, Y_TP, i).wait_recv()
         hc[rows, :] += bs[rows, :] + br[rows, :]
-    pump(BATCHES * 2 * RING)
+    pump(len(starts) * 2 * RING)
     finish()
     y_sent(br, Y_TP)
 
@@ -554,7 +570,7 @@
     T, D = tokens.shape
     L, F = query_weight.shape[1], up_weight.shape[1]
     anywhere, vmem = pl.BlockSpec(memory_space=pl.ANY), pl.BlockSpec(memory_space=pltpu.VMEM)
-    sub = 3 * F // BATCHES
+    NB = len(sub_batches(F)[0])
     dma = pltpu.SemaphoreType.DMA
     V = pltpu.VMEM
     G, hc, hid, term, smt = pl.pallas_call(
@@ -576,9 +592,9 @@
             V((2 * T, L), bf16), V((2 * L, T), bf16), V((L, T), bf16),
             V((T, 8), f32), V((T, 8), f32),
             V((4, 16, D), f32), V((4, 16, D), f32),
-            V((BATCHES, sub // 2, D), f32), V((BATCHES, RING - 1, sub // 2 // RING, D), f32),
+            V((3 * F // 2, D), f32), V((3 * F // 2 // RING * (RING - 1), D), f32),
             dma((22,)), dma((14,)), dma((17,)), dma, dma((4,)), dma((4,)), dma((4,)),
-            dma((BATCHES,)), dma((BATCHES,)), dma, dma((BATCHES, RING)), dma, dma, pltpu.SemaphoreType.REGULAR((BATCHES,)),
+            dma((NB,)), dma((NB,)), dma, dma((NB, RING)), dma, dma, pltpu.SemaphoreType.REGULAR((NB,)),
         ],
         compiler_params=pltpu.CompilerParams(
             collective_id=0, has_side_effects=True, vmem_limit_bytes=VMEM_LIMIT

time: 217 us -> 214 us (0.986)
    pallas_call x1, Pallas kernels: 209 us -> 207 us  [per_device(): pl.pallas_call(kernel, out_shape=[V((3 * F, D), f32), V((T, D), f32), V((...]
where the time goes in v5:
time: 214 us
  Pallas kernels  213 us (100%)
    pallas_call x1, Pallas kernels, per_device(): pl.pallas_call(kernel, out_shape=[V((3 * F, D), f32), V((T, D), f32), V((...  207 us
    pallas_call x1, Pallas kernels, per_device(): pl.pallas_call(spread, out_shape=[jax.ShapeDtypeStruct((T, D), bf16), vt,...  5.98 us

profile of v5, /device:TPU:0, one launch (start us, length us, event | category | flops | bytes accessed | tf_op | source)
XLA Modules:
  0.0 214.1 jit_solution(6351485446917051417)
XLA Ops:
  1.3 206.6 %shard_map.365 = (f32[4608,768]{1,0:T(8,128)S(1)}, f32[512,768]{1,0:T(8,128)S(1)}, bf16[512,768]{1,0:T(8,128)(2,1)S(1)}, f32[8,512]{1,0:T(8,128)S(1)}, f32[16,768]{1,0:T(8,128)S(1)}) custom-call(bf16[512,768]{1,0:T(8,128)(2,1)} %tokens.1, s32[1,512]{1,0:T(1,128)} %i_seg.1, s32[1,512]{1,0:T(1,128)} %i_pad.1, f32[512]{0:T(512)} %tcot.1, bf16[384]{0:T(512)(128)(2,1)} %i_qb.1, ...), custom_call_target="tpu_custom_call" | custom-call | tf_op jit(solution)/shard_map/pallas_call | solution.py:576
  207.9 6.0 %shard_map.366 = (bf16[512,768]{1,0:T(8,128)(2,1)}, f32[512]{0:T(512)}, f32[512,768]{1,0:T(8,128)}, f32[768,384]{1,0:T(8,128)}, f32[384]{0:T(512)}, /*index=5*/f...) custom-call(f32[4608,768]{1,0:T(8,128)S(1)} %get-tuple-element.25.G,, ...), custom_call_target="tpu_custom_call" | custom-call | tf_op jit(solution)/shard_map/pallas_call | solution.py:610

commit v6 on v5

--- a/solution.py
+++ b/solution.py
@@ -91,21 +91,20 @@
             src_ref=src, dst_ref=dst, send_sem=ss, recv_sem=rr, device_id=dev, device_id_type=MESH
         )
 
-    pairs = [
-        (wo, wo_v), (tokens, tok_v), (wq, wq_v), (wk, wk_v), (wv, wv_v), (wu, wu_v), (wd, wd_v), (hcot, hc),
-        (tcot, v_tcot), (i_qb, v_qb), (i_vb, v_vb), (i_ob, v_ob), (i_g1, v_g1), (i_s1, v_s1), (i_ub, v_ub), (i_db, v_db),
-        (i_g2, v_g2), (i_s2, v_s2), (i_tw, v_tw), (i_tb, v_tb), (i_seg, seg), (i_pad, pad),
-    ]
-    loads = [pltpu.make_async_copy(a, b, ld_sem.at[i]) for i, (a, b) in enumerate(pairs)]
-    for c in loads:
-        c.start()
-    L_WO, L_TOK, L_WQ, L_WK, L_WV, L_WU, L_WD, L_HC, *L_VEC = loads
-
     peers = (YN, SIB, NXT, PRV, XN, Z1, Z2)
     bar = pltpu.get_barrier_semaphore()
     for d in peers:
         pl.semaphore_signal(bar, inc=1, device_id=d, device_id_type=MESH)
-    pl.semaphore_wait(bar, len(peers))
+
+    pairs = [
+        (tokens, tok_v), (wq, wq_v), (wk, wk_v), (wv, wv_v), (wo, wo_v), (tcot, v_tcot), (i_qb, v_qb), (i_vb, v_vb),
+        (i_ob, v_ob), (i_g1, v_g1), (i_s1, v_s1), (i_ub, v_ub), (i_db, v_db), (i_g2, v_g2), (i_s2, v_s2), (i_tw, v_tw),
+        (i_tb, v_tb), (i_seg, seg), (i_pad, pad), (wu, wu_v), (wd, wd_v), (hcot, hc),
+    ]
+    loads = [pltpu.make_async_copy(a, b, ld_sem.at[i]) for i, (a, b) in enumerate(pairs)]
+    L_TOK, L_WQ, L_WK, L_WV, L_WO, *L_VEC, L_WU, L_WD, L_HC = loads
+    for c in loads[:-3]:
+        c.start()
 
     r_wor = 4 * SUB
     r_wos = r_wor + L
@@ -118,8 +117,6 @@
         return G.at[pl.ds(pl.multiple_of(r_wor + ((az * 2 + ax) * 2 + ac) * SH, 16), SH)]
 
     zp = z % 2
-    L_WO.wait()
-    G[r_wos : r_wos + SH, :] = wo_v[pl.ds(pl.multiple_of(((zp * 2 + x) * 2 + core) * SH, 16), SH), :].astype(f32)
 
     def wo_copy(k):
         ax, az = ((x, zp), (x, zp), (x, zp), (1 - x, zp), (x, zp), (1 - x, zp), (x, 1 - zp), (1 - x, 1 - zp))[k]
@@ -127,8 +124,6 @@
         if k == 0:
             return rc(G.at[pl.ds(r_wos, SH)], place, y_s.at[0], y_r.at[0], YN)
         return rc(place, place, wo_s, wo_r.at[min(k, 4) - 1], (XN, Z1, Z1, SIB, SIB, SIB, SIB)[k - 1])
-
-    wo_copy(0).start()
 
     for c in L_VEC:
         c.wait()
@@ -162,6 +157,13 @@
     vn[...] = vv
     vT[...] = vv.T
 
+    for c in loads[-3:]:
+        c.start()
+    L_WO.wait()
+    G[r_wos : r_wos + SH, :] = wo_v[pl.ds(pl.multiple_of(((zp * 2 + x) * 2 + core) * SH, 16), SH), :].astype(f32)
+    pl.semaphore_wait(bar, len(peers))
+    wo_copy(0).start()
+
     segf, padf = seg[...].astype(f32), pad[...].astype(f32)
     rows8 = jnp.concatenate([segf, padf, v_tcot[...].reshape(1, T), jnp.zeros((5, T), f32)], axis=0)
     col[...] = rows8.T
@@ -172,13 +174,17 @@
         allowed = same & ((col[:, 1:2] == 0.0) | (ki == qi))
         G[r_bias : r_bias + T, qc * CH : (qc + 1) * CH] = jnp.where(allowed, 0.0, -1e9)
 
-    Y_CTX, Y_BR, Y_FP, Y_TP = 1, 1 + NPC, 1 + 2 * NPC, 1 + 3 * NPC
+    Y_CTX, Y_BR, Y_FP, Y_TP, Y_PART = 1, 1 + NPC, 1 + 2 * NPC, 1 + 3 * NPC, 1 + 4 * NPC
 
     def span(i):
         return pl.ds(pl.multiple_of(i * PC, PC), PC)
 
     def ctx_copy(i):
         return rc(G.at[pl.ds(r_cs, L), span(i)], G.at[pl.ds(r_cr, L), span(i)], y_s.at[1], y_r.at[Y_CTX + i], YN)
+
+    def ctx_part(hp):
+        rows = [pl.ds(pl.multiple_of(r + hp * 128, 128), 128) for r in (r_cs, r_cr)]
+        return rc(G.at[rows[0], span(0)], G.at[rows[1], span(0)], y_s.at[1], y_r.at[Y_PART + hp], YN)
 
     def attend(i):
         def body(hp, _):
@@ -193,13 +199,16 @@
                 c = nn(vT[pl.ds(head, HEAD_DIM), :], p).astype(bf16)
                 ctxT[pl.ds(head, HEAD_DIM), span(i)] = c
                 G[pl.ds(pl.multiple_of(r_cs + head, HEAD_DIM), HEAD_DIM), span(i)] = c.astype(f32)
+            if i == 0:
+                ctx_part(hp).start()
             return 0
 
         lax.fori_loop(0, NP, body, 0)
 
     for i in range(NPC):
         attend(i)
-        ctx_copy(i).start()
+        if i > 0:
+            ctx_copy(i).start()
         if i == 1:
             wo_copy(0).wait_recv()
             for k in (1, 2, 4):
@@ -230,7 +239,16 @@
 
     def forward(i, _):
         rows = span(i)
-        ctx_copy(i).wait_recv()
+
+        @pl.when(i == 0)
+        def _():
+            for hp in range(NP):
+                ctx_part(hp).wait_recv()
+
+        @pl.when(i > 0)
+        def _():
+            ctx_copy(i).wait_recv()
+
         other = G[r_cr : r_cr + L, rows].astype(bf16)
         res = tok_v[rows, :].astype(f32) + (tn(ctxT[:, rows], wo_v[...]) + tn(other, woo_v[...])) + vec[V_OB : V_OB + 1, :]
         cen = res - rowmean(res)
@@ -504,17 +522,28 @@
     sm[0, G_QV : G_QV + 1, 0:L] = colsum(dq[...].astype(f32))
     sm[0, G_QV : G_QV + 1, L : 2 * L] = colsum(dv[...].astype(f32))
 
+    mine_sm, other_sm = pl.ds(pl.multiple_of(core * 8, 8), 8), pl.ds(pl.multiple_of((1 - core) * 8, 8), 8)
+
     def sm_copy(k):
-        return rc(sm.at[k], smr.at[k], sm_s.at[k], sm_r.at[k], (SIB, XN, Z1, Z2)[k])
+        if k == 0:
+            return rc(sm.at[0], smr.at[0], sm_s.at[0], sm_r.at[0], SIB)
+        if k == 4:
+            return rc(sm.at[4, mine_sm], smr.at[4, mine_sm], sm_s.at[4], sm_r.at[4], SIB)
+        return rc(sm.at[k, mine_sm], smr.at[k, mine_sm], sm_s.at[k], sm_r.at[k], (XN, Z1, Z2)[k - 1])
 
     for k in range(4):
         sm_copy(k).start()
         pump(PUMPS[6])
         sm_copy(k).wait()
-        if k < 3:
-            sm[k + 1] = sm[k] + smr[k]
+        if k == 0:
+            sm[1] = sm[0] + smr[0]
         else:
-            smt[...] = sm[k] + smr[k]
+            sm[k + 1, mine_sm] = sm[k, mine_sm] + smr[k, mine_sm]
+    sm_copy(4).start()
+    smt[mine_sm, :] = sm[4, mine_sm]
+    pump(2)
+    sm_copy(4).wait()
+    smt[other_sm, :] = smr[4, other_sm]
     o_term[...] = trm[...].T
 
     for i in range(NPC):
@@ -591,9 +620,9 @@
             V((T, D), bf16), V((T, F), bf16),
             V((2 * T, L), bf16), V((2 * L, T), bf16), V((L, T), bf16),
             V((T, 8), f32), V((T, 8), f32),
-            V((4, 16, D), f32), V((4, 16, D), f32),
+            V((5, 16, D), f32), V((5, 16, D), f32),
             V((3 * F // 2, D), f32), V((3 * F // 2 // RING * (RING - 1), D), f32),
-            dma((22,)), dma((14,)), dma((17,)), dma, dma((4,)), dma((4,)), dma((4,)),
+            dma((22,)), dma((14,)), dma((17 + L // 128,)), dma, dma((4,)), dma((5,)), dma((5,)),
             dma((NB,)), dma((NB,)), dma, dma((NB, RING)), dma, dma, pltpu.SemaphoreType.REGULAR((NB,)),
         ],
         compiler_params=pltpu.CompilerParams(

time: 214 us -> 213 us (level)
  no operation moved by 1% of the time
where the time goes in v6:
time: 213 us; the launch traced here: 212 us
  Pallas kernels  211 us (99%)
    pallas_call x1, Pallas kernels, per_device(): pl.pallas_call(kernel, out_shape=[V((3 * F, D), f32), V((T, D), f32), V((...  205 us
    pallas_call x1, Pallas kernels, per_device(): pl.pallas_call(spread, out_shape=[jax.ShapeDtypeStruct((T, D), bf16), vt,...  5.98 us

profile of v6, /device:TPU:0, one launch (start us, length us, event | category | flops | bytes accessed | tf_op | source)
XLA Modules:
  0.0 212.3 jit_solution(8763893706223276335)
XLA Ops:
  1.3 204.9 %shard_map.365 = (f32[4608,768]{1,0:T(8,128)S(1)}, f32[512,768]{1,0:T(8,128)S(1)}, bf16[512,768]{1,0:T(8,128)(2,1)S(1)}, f32[8,512]{1,0:T(8,128)S(1)}, f32[16,768]{1,0:T(8,128)S(1)}) custom-call(bf16[512,768]{1,0:T(8,128)(2,1)} %tokens.1, s32[1,512]{1,0:T(1,128)} %i_seg.1, s32[1,512]{1,0:T(1,128)} %i_pad.1, f32[512]{0:T(512)} %tcot.1, bf16[384]{0:T(512)(128)(2,1)} %i_qb.1, ...), custom_call_target="tpu_custom_call" | custom-call | tf_op jit(solution)/shard_map/pallas_call | solution.py:605
  206.2 6.0 %shard_map.366 = (bf16[512,768]{1,0:T(8,128)(2,1)}, f32[512]{0:T(512)}, f32[512,768]{1,0:T(8,128)}, f32[768,384]{1,0:T(8,128)}, f32[384]{0:T(512)}, /*index=5*/f...) custom-call(f32[4608,768]{1,0:T(8,128)S(1)} %get-tuple-element.25.G,, ...), custom_call_target="tpu_custom_call" | custom-call | tf_op jit(solution)/shard_map/pallas_call | solution.py:639

commit v7 on v6

--- a/solution.py
+++ b/solution.py
@@ -53,8 +53,8 @@
     v_tcot, v_qb, v_vb, v_ob, v_g1, v_s1, v_ub, v_db, v_g2, v_s2, v_tw, v_tb, seg, pad, vec, ubv,
     tok_v, wq_v, wk_v, wv_v, wo_v, woo_v, wu_v, wd_v,
     kn, vn, kT, vT, qz, qTz, pm, ctxT, xh, rs, first_v, fl, gp, act, bs, br, fr, db, du,
-    dcz, dcTz, dqT, col, trm, sm, smr, S, R,
-    ld_sem, y_s, y_r, wo_s, wo_r, sm_s, sm_r, sib_s, sib_r, ring_s, ring_r, fw_s, fw_r, free_sib,
+    dcz, dcTz, dqT, col, trm, sm, smr, S, S1, R,
+    ld_sem, y_s, y_r, wo_s, wo_r, sm_s, sm_r, sib_s, sib_r, one_s, one_r, ring_s, ring_r, fw_s, fw_r, free_sib,
 ):
     T, D = tokens.shape
     L, F = wq.shape[1], wu.shape[1]
@@ -367,8 +367,14 @@
         src = G.at[pl.ds(pl.multiple_of(starts[b] + (1 - core) * half, 8), half)]
         return rc(src, S.at[pl.ds(starts[b] // 2, half)], sib_s.at[b], sib_r.at[b], SIB)
 
+    def one_copy(b):
+        size = sizes[b] // 2 // RING
+        begin = starts[b] + (1 - core) * (sizes[b] // 2) + (RING - vp) % RING * size
+        return rc(G.at[pl.ds(pl.multiple_of(begin, 8), size)], S1.at[b], one_s.at[b], one_r.at[b], SIB)
+
     def rs_copy(b, k):
-        return rc(own(b, vp) if k == 0 else slot(b, k - 1), slot(b, k), ring_s, ring_r.at[b, k], NXT)
+        begin = S1.at[b] if b < len(DOWN) else own(b, vp)
+        return rc(begin if k == 0 else slot(b, k - 1), slot(b, k), ring_s, ring_r.at[b, k], NXT)
 
     def ag_copy(b, k, back):
         rows = G.at[chunk(b, (vp + 1 - back - k + RING) % RING)]
@@ -379,14 +385,21 @@
         return rc(rows, rows, fw_s, fw_r, SIB)
 
     def event(b, e):
+        early = b < len(DOWN)
+        if e == (2 if early else 1):
+            sib_copy(b).wait()
+            if early:
+                one_copy(b).wait_send()
+            pl.semaphore_signal(free_sib.at[b], inc=1, device_id=SIB, device_id_type=MESH)
         if e == 0:
-            sib_copy(b).start()
+            (one_copy if early else sib_copy)(b).start()
         elif e == 1:
-            sib_copy(b).wait_recv()
-            own(b, vp)[...] += G[chunk(b, vp), :]
+            if early:
+                one_copy(b).wait_recv()
+                S1[b] += G[chunk(b, vp), :]
+            else:
+                own(b, vp)[...] += G[chunk(b, vp), :]
             rs_copy(b, 0).start()
-            sib_copy(b).wait_send()
-            pl.semaphore_signal(free_sib.at[b], inc=1, device_id=SIB, device_id_type=MESH)
         elif e < RING:
             k = e - 1
             rs_copy(b, k - 1).wait_recv()
@@ -438,6 +451,8 @@
     for b in range(4):
         G[b * SUB : (b + 1) * SUB, :] += down_grad(b, last)
         complete((b + 1) * SUB)
+    for b in range(len(DOWN)):
+        sib_copy(b).start()
     ffn_back(NPC - 1, lambda: pump(PUMPS[0]))
     for b in range(4):
         G[(4 + b) * SUB : (5 + b) * SUB, :] += up_grad(b, last)
@@ -621,9 +636,9 @@
             V((2 * T, L), bf16), V((2 * L, T), bf16), V((L, T), bf16),
             V((T, 8), f32), V((T, 8), f32),
             V((5, 16, D), f32), V((5, 16, D), f32),
-            V((3 * F // 2, D), f32), V((3 * F // 2 // RING * (RING - 1), D), f32),
+            V((3 * F // 2, D), f32), V((len(DOWN), DOWN[0] * F // 12 // 2 // RING, D), f32), V((3 * F // 2 // RING * (RING - 1), D), f32),
             dma((22,)), dma((14,)), dma((17 + L // 128,)), dma, dma((4,)), dma((5,)), dma((5,)),
-            dma((NB,)), dma((NB,)), dma, dma((NB, RING)), dma, dma, pltpu.SemaphoreType.REGULAR((NB,)),
+            dma((NB,)), dma((NB,)), dma((len(DOWN),)), dma((len(DOWN),)), dma, dma((NB, RING)), dma, dma, pltpu.SemaphoreType.REGULAR((NB,)),
         ],
         compiler_params=pltpu.CompilerParams(
             collective_id=0, has_side_effects=True, vmem_limit_bytes=VMEM_LIMIT

time: 213 us -> 212 us (level)
  no operation moved by 1% of the time
where the time goes in v7:
time: 212 us
  Pallas kernels  211 us (100%)
    pallas_call x1, Pallas kernels, per_device(): pl.pallas_call(kernel, out_shape=[V((3 * F, D), f32), V((T, D), f32), V((...  205 us
    pallas_call x1, Pallas kernels, per_device(): pl.pallas_call(spread, out_shape=[jax.ShapeDtypeStruct((T, D), bf16), vt,...  5.98 us

profile of v7, /device:TPU:0, one launch (start us, length us, event | category | flops | bytes accessed | tf_op | source)
XLA Modules:
  0.0 212.3 jit_solution(32611169512240478)
XLA Ops:
  1.3 204.8 %shard_map.365 = (f32[4608,768]{1,0:T(8,128)S(1)}, f32[512,768]{1,0:T(8,128)S(1)}, bf16[512,768]{1,0:T(8,128)(2,1)S(1)}, f32[8,512]{1,0:T(8,128)S(1)}, f32[16,768]{1,0:T(8,128)S(1)}) custom-call(bf16[512,768]{1,0:T(8,128)(2,1)} %tokens.1, s32[1,512]{1,0:T(1,128)} %i_seg.1, s32[1,512]{1,0:T(1,128)} %i_pad.1, f32[512]{0:T(512)} %tcot.1, bf16[384]{0:T(512)(128)(2,1)} %i_qb.1, ...), custom_call_target="tpu_custom_call" | custom-call | tf_op jit(solution)/shard_map/pallas_call | solution.py:620
  206.1 6.0 %shard_map.366 = (bf16[512,768]{1,0:T(8,128)(2,1)}, f32[512]{0:T(512)}, f32[512,768]{1,0:T(8,128)}, f32[768,384]{1,0:T(8,128)}, f32[384]{0:T(512)}, /*index=5*/f...) custom-call(f32[4608,768]{1,0:T(8,128)S(1)} %get-tuple-element.25.G,, ...), custom_call_target="tpu_custom_call" | custom-call | tf_op jit(solution)/shard_map/pallas_call | solution.py:654
